TPU v7x, 256 devices: a whole 4x4x8 slice. The times are simulated.
256 devices in a mesh: section: 8 (over z), ep: 32 (over y, x, core).
Axes of the slice: x: 4, y: 4, z: 8, core: 2. Of those that a mesh axis runs over, the one named last changes fastest.
Arguments:
- arriving: bfloat16 [8, 2048, 3072], P('section', 'ep'), may hold values from -6 to 6
- top_grad: bfloat16 [1, 2048, 3072], P(None, 'ep'), may hold values from -6 to 6
- expert_ids: int32 [8, 2, 2048, 2], P('section'), may hold values from 0 to 3, all different within a row; in each aligned block of 64 rows (0 to 63, 64 to 127, ..., all dimensions but the last counted through in order) at most 36 rows name the same one
- first_share: float32 [8, 2, 2048], P('section', None, 'ep'), may hold values from 0.5 to 0.95
- out_gap: bfloat16 [8, 2, 2048, 3072], P('section', None, 'ep'), may hold values from -6 to 6
- router_weight: float32 [8, 4, 3072], P('section'), may hold values from -0.75 to 0.75
- down_weight: bfloat16 [8, 32768, 3072], P('section', 'ep'), may hold values from -0.109375 to 0.109375
Outputs:
- departing: bfloat16 [8, 2, 2048, 3072], P('section', None, 'ep')
- hidden_grad: bfloat16 [8, 2, 36864, 1024], P('section', None, 'ep')
Inputs may be any that keep to these rules, and one draw needn't show every extreme that they name: `expert_ids`: A token's two ids differ; within one step each device's 64 tokens name any one expert at most 36 times.
All inputs are finite; a program needn't handle non-finite values.
Results may differ from a plain program's by a relative error of at most 0.0054.
Values may be sent and summed in bfloat16 or wider, within the bound.
No kernel may reach another device: no remote copies, remote signals or barrier semaphores. Data moves between devices by JAX's collectives and lax.ppermute only.
A program may use at most 128 MiB of HBM per device.

v0:
```python
import functools

import jax
import jax.numpy as jnp
import numpy as np
from jax import lax
from jax.experimental import pallas as pl
from jax.experimental.pallas import tpu as pltpu
from jax.sharding import PartitionSpec as P

TICKS = 2
CAP = 36
XS, YS, CORES = 4, 4, 2
EP = XS * YS * CORES
TOKENS = 64
D = 3072
HID = 1024
MAXP = EP * CAP
BLOCK = YS * CAP
HEAD = 80
DYS = (0, 1, 3, 2)
DXS = (0, 1, 3, 2)
WIDE = 256
VMEM = pl.BlockSpec(memory_space=pltpu.VMEM)
ANY = pl.BlockSpec(memory_space=pl.ANY)
NT = (((1,), (1,)), ((), ()))


def hop(shard, dy=0, dx=0, dc=0):
    pairs = []
    for y in range(YS):
        for x in range(XS):
            for c in range(CORES):
                to = (((y + dy) % YS) * XS + (x + dx) % XS) * CORES + (c + dc) % CORES
                pairs.append(((y * XS + x) * CORES + c, to))
    return lax.ppermute(shard, "ep", pairs)


def down(shard):
    n = lax.axis_size("section")
    return lax.ppermute(shard, "section", [(i, i - 1) for i in range(1, n)])


def own_ids_of(ids_ref, moment, me):
    both = ids_ref[moment, :, pl.ds(pl.multiple_of((me // 2) * 128, 128), 128)].astype(jnp.float32)
    return jnp.where(me % 2 == 0, both[:, :TOKENS], both[:, TOKENS:])


def gradient_of(refs):
    if len(refs) == 1:
        return refs[0][...]
    top, moved = refs
    last = lax.axis_index("section") == lax.axis_size("section") - 1
    return jnp.where(last, top[...], moved[...])


def route_kernel(moment, ids_ref, share_ref, *refs):
    grads, outs = refs[:-YS], refs[-YS:]
    me = lax.axis_index("ep")
    my_y = (me // (XS * CORES)).astype(jnp.float32)
    own = own_ids_of(ids_ref, moment, me)
    first, second = own[0:1], own[1:2]
    experts = lax.broadcasted_iota(jnp.int32, (8, TOKENS), 0).astype(jnp.float32)
    is_first, is_second = experts == first, experts == second
    chosen = (is_first | is_second).astype(jnp.float32).astype(jnp.bfloat16)
    before = lax.broadcasted_iota(jnp.int32, (TOKENS, TOKENS), 0) < lax.broadcasted_iota(
        jnp.int32, (TOKENS, TOKENS), 1
    )
    ranks = jnp.dot(chosen, before.astype(jnp.float32).astype(jnp.bfloat16), preferred_element_type=jnp.float32)

    def place(expert, mask):
        relative = expert - my_y
        relative = jnp.where(relative < 0, relative + YS, relative)
        return relative * CAP + jnp.sum(jnp.where(mask, ranks, 0.0), 0, keepdims=True)

    place_1, place_2 = place(first, is_first), place(second, is_second)
    share = share_ref[moment : moment + 1, :]
    gradient = gradient_of(grads)
    slots = lax.broadcasted_iota(jnp.int32, (CAP, TOKENS), 0).astype(jnp.float32)
    for j in range(YS):
        one, two = slots + j * CAP == place_1, slots + j * CAP == place_2
        weight = jnp.sum(jnp.where(one, share, 0.0) + jnp.where(two, 1.0 - share, 0.0), 1, keepdims=True)
        placing = (one | two).astype(jnp.float32).astype(jnp.bfloat16)
        rows = jnp.dot(placing, gradient, preferred_element_type=jnp.float32)
        outs[j][...] = (rows * weight).astype(jnp.bfloat16)


def route(moment, ids, share, grads):
    return pl.pallas_call(
        functools.partial(route_kernel, moment),
        out_shape=[jax.ShapeDtypeStruct((CAP, D), jnp.bfloat16)] * YS,
        in_specs=[VMEM] * (2 + len(grads)),
        out_specs=[VMEM] * YS,
        compiler_params=pltpu.CompilerParams(vmem_limit_bytes=16 << 20),
        cost_estimate=pl.CostEstimate(flops=2 * BLOCK * TOKENS * D, bytes_accessed=2 * 208 * D, transcendentals=0),
        name="route",
    )(ids, share, *grads)


def router_kernel(moment, count, ids_ref, share_ref, router_ref, gap_ref, *refs):
    grads, outs = refs[:count], refs[-2:]
    me = lax.axis_index("ep")
    own = own_ids_of(ids_ref, moment, me)
    eye = lax.broadcasted_iota(jnp.int32, (TOKENS, TOKENS), 0) == lax.broadcasted_iota(
        jnp.int32, (TOKENS, TOKENS), 1
    )

    def upright(row):
        return jnp.sum(jnp.where(eye, row, 0.0), 1, keepdims=True)

    first, second = upright(own[0:1]), upright(own[1:2])
    share = upright(share_ref[moment : moment + 1, :])
    gradient = gradient_of(grads).astype(jnp.float32)
    gap_dot = jnp.sum(gradient * gap_ref[0].astype(jnp.float32), 1, keepdims=True)
    logit_grad = share * (1.0 - share) * gap_dot
    term = jnp.zeros((TOKENS, D), jnp.float32)
    for e in range(YS):
        sign = jnp.where(first == e, 1.0, 0.0) - jnp.where(second == e, 1.0, 0.0)
        term = term + (logit_grad * sign) * router_ref[e : e + 1, :]
    departing = (gradient + term).astype(jnp.bfloat16)
    outs[0][0] = departing
    outs[1][...] = departing


def router(moment, ids, share, router_rows, gap, grads, departs):
    more = [] if departs is None else [departs]
    return pl.pallas_call(
        functools.partial(router_kernel, moment, len(grads)),
        grid=(1,),
        out_shape=[
            jax.ShapeDtypeStruct((TICKS, TOKENS, D), jnp.bfloat16),
            jax.ShapeDtypeStruct((TOKENS, D), jnp.bfloat16),
        ],
        in_specs=[VMEM] * 3
        + [pl.BlockSpec((1, TOKENS, D), lambda i: (moment, 0, 0))]
        + [VMEM] * len(grads)
        + [ANY] * len(more),
        out_specs=[pl.BlockSpec((1, TOKENS, D), lambda i: (moment, 0, 0)), VMEM],
        input_output_aliases={4 + len(grads): 0} if more else {},
        compiler_params=pltpu.CompilerParams(vmem_limit_bytes=16 << 20),
        cost_estimate=pl.CostEstimate(flops=12 * TOKENS * D, bytes_accessed=2 * 256 * D, transcendentals=0),
        name="router",
    )(ids, share, router_rows, gap, *grads, *more)


def experts_kernel(moment, sizes, earlier, ids_ref, table_ref, *refs):
    count = len(sizes)
    pieces, down_ref = refs[:count], refs[count]
    out_ref, rows_ref, placing_ref, sems = refs[-4:]
    total = sum(sizes)

    @pl.when(pl.program_id(0) == 0)
    def _():
        copies, begin = [], 0
        for i, size in enumerate(sizes):
            copies.append(pltpu.make_async_copy(pieces[i], rows_ref.at[pl.ds(begin, size)], sems.at[i]))
            copies[-1].start()
            begin += size
        me = lax.axis_index("ep")
        my_y, my_x, my_c = me // (XS * CORES), (me // CORES) % XS, me % CORES
        named = (ids_ref[moment] == my_y).astype(jnp.float32)
        named = jnp.broadcast_to(named[0:1] + named[1:2], (8, EP * TOKENS)).astype(jnp.bfloat16)
        owner = lax.broadcasted_iota(jnp.int32, (EP, EP * TOKENS), 1) // TOKENS
        owned = owner == lax.broadcasted_iota(jnp.int32, (EP, EP * TOKENS), 0)
        counts = lax.dot_general(
            named, owned.astype(jnp.float32).astype(jnp.bfloat16), NT, preferred_element_type=jnp.float32
        ).astype(jnp.bfloat16)
        table = table_ref[...]
        source = (
            ((my_y - table[0:1]) & (YS - 1)) * (XS * CORES)
            + ((my_x - table[1:2]) & (XS - 1)) * CORES
            + ((my_c - table[2:3]) & (CORES - 1))
        )
        slot = table[3:4].astype(jnp.float32)
        device = lax.broadcasted_iota(jnp.int32, (EP, total), 0)
        ahead = (device < source).astype(jnp.float32).astype(jnp.bfloat16)
        itself = (device == source).astype(jnp.float32).astype(jnp.bfloat16)
        offset = jnp.dot(counts, ahead, preferred_element_type=jnp.float32)[0:1]
        amount = jnp.dot(counts, itself, preferred_element_type=jnp.float32)[0:1]
        target = jnp.where(slot < amount, offset + slot, -1.0).astype(jnp.int32)
        step = 128

        @pl.loop(0, MAXP // step)
        def _(k):
            at = pl.multiple_of(k * step, step)
            here = lax.broadcasted_iota(jnp.int32, (step, total), 0) + at
            placing_ref[pl.ds(at, step), :] = (here == target).astype(jnp.float32).astype(jnp.bfloat16)

        for copy in copies:
            copy.wait()

    product = lax.dot_general(rows_ref[...], down_ref[...], NT, preferred_element_type=jnp.float32)
    placed = jnp.dot(placing_ref[...], product.astype(jnp.bfloat16), preferred_element_type=jnp.float32)
    if earlier:
        placed = placed + refs[count + 1][0].astype(jnp.float32)
    out_ref[0] = placed.astype(jnp.bfloat16)


def experts(moment, ids, groups, down_rows, hidden, earlier):
    pieces, columns = [], []
    for dx, dc, parts in groups:
        pieces += parts
        for dy in DYS:
            columns += [(dy, dx, dc, slot) for slot in range(CAP)]
    table = np.zeros((8, len(columns)), np.int32)
    table[:4] = np.array(columns, np.int32).T
    total = len(columns)
    sizes = tuple(p.shape[0] for p in pieces)
    block = pl.BlockSpec((1, MAXP, WIDE), lambda n: (moment, 0, n))
    more = [] if hidden is None else [hidden]
    return pl.pallas_call(
        functools.partial(experts_kernel, moment, sizes, earlier),
        grid=(HID // WIDE,),
        out_shape=jax.ShapeDtypeStruct((TICKS, MAXP, HID), jnp.bfloat16),
        in_specs=[VMEM, VMEM]
        + [ANY] * len(pieces)
        + [pl.BlockSpec((WIDE, D), lambda n: (n, 0))]
        + ([block if earlier else ANY] if more else []),
        out_specs=block,
        scratch_shapes=[
            pltpu.VMEM((total, D), jnp.bfloat16),
            pltpu.VMEM((MAXP, total), jnp.bfloat16),
            pltpu.SemaphoreType.DMA((len(pieces),)),
        ],
        input_output_aliases={3 + len(pieces): 0} if more else {},
        compiler_params=pltpu.CompilerParams(vmem_limit_bytes=32 << 20),
        cost_estimate=pl.CostEstimate(
            flops=2 * total * HID * (D + MAXP),
            bytes_accessed=2 * (total * D + HID * D + MAXP * HID * (2 if earlier else 1)),
            transcendentals=0,
        ),
        name="experts",
    )(ids, jnp.asarray(table), *pieces, down_rows, *more)


def exchange(parts):
    r1, r3, r2 = hop(parts[1], dy=1), hop(parts[3], dy=3), hop(parts[2], dy=2)
    split = HEAD - 2 * CAP
    head = jnp.concatenate([parts[0], r1, r3[:split]], 0)
    tail = jnp.concatenate([r3[split:], r2], 0)
    got = {0: (head, tail)}
    got[1] = (hop(head, dx=1), hop(tail, dx=1))
    got[3] = (hop(head, dx=3), hop(tail, dx=3))
    got[2] = (hop(got[1][0], dx=1), hop(got[3][1], dx=3))
    out = {}
    for dx in DXS:
        out[dx, 0] = got[dx]
        out[dx, 1] = tuple(hop(p, dc=1) for p in got[dx])
    return out


def local(arriving, top_grad, expert_ids, first_share, out_gap, router_weight, down_weight):
    ids = jnp.swapaxes(expert_ids[0], 1, 2)
    share, gap, router_rows, down_rows = first_share[0], out_gap[0], router_weight[0], down_weight[0]
    grads = [arriving[0]]
    departs = hidden = None
    for moment in range(TICKS):
        parts = route(moment, ids, share, grads)
        departs, departing = router(moment, ids, share, router_rows, gap, grads, departs)
        got = exchange(parts)
        early = [(dx, dc, got[dx, dc]) for dx in DXS[:3] for dc in range(CORES)]
        late = [(dx, dc, got[dx, dc]) for dx in DXS[3:] for dc in range(CORES)]
        hidden = experts(moment, ids, early, down_rows, hidden, False)
        hidden = experts(moment, ids, late, down_rows, hidden, True)
        if moment + 1 < TICKS:
            grads = [top_grad[moment], down(departing)]
    return departs[None], hidden[None]


def solution(mesh):
    placed = (
        P("section", "ep", None),
        P(None, "ep", None),
        P("section", None, None, None),
        P("section", None, "ep"),
        P("section", None, "ep", None),
        P("section", None, None),
        P("section", "ep", None),
    )
    return jax.shard_map(
        local,
        mesh=mesh,
        in_specs=placed,
        out_specs=(P("section", None, "ep", None), P("section", None, "ep", None)),
        check_vma=False,
    )
```

profile of v0, /device:TPU:249, one launch (start us, length us, event | category | flops | bytes accessed | tf_op | source)
XLA Modules:
  0.0 141.9 jit_solution(14351488586168252337)
XLA Ops:
  5.0 1.6 %copy-done.1 = bf16[1,2,64,3072]{3,2,1,0:T(8,128)(2,1)S(1)} copy-done((bf16[1,2,64,3072]{3,2,1,0:T(8,128)(2,1)S(1)}, bf16[1,2,64,3072]{3,2,1,0:T(8,128)(2,1)}, u32[]{:S(2)}) %copy-start.1) | copy-done | bytes 786456
  9.6 2.7 %collective-permute-start = (bf16[64,3072]{1,0:T(8,128)(2,1)S(1)}, bf16[64,3072]{1,0:T(8,128)(2,1)S(1)}, u32[]{:S(2)}, u32[]{:S(2)}) collective-permute-start(bf16[64,3072]{1,0:T(8,128)(2,1)S(1)} %get-tuple-element.13), channel_id=1, source_target_pairs={{32,0},{64,32},{96,64},{128,96},{160,128},{192,160},{224,192},{33,... | collective-permute-start | bytes 1179656 | tf_op jit(solution)/shard_map/ppermute | solution.py:41
  12.3 4.9 %collective-permute-done.19 = bf16[36,3072]{1,0:T(8,128)(2,1)S(1)} collective-permute-done((bf16[36,3072]{1,0:T(8,128)(2,1)S(1)}, bf16[36,3072]{1,0:T(8,128)(2,1)S(1)}, u32[]{:S(2)}, u32[]{:S(2)}) %collective-permute-start.19) | collective-permute-done | bytes 221216 | tf_op jit(solution)/shard_map/ppermute | solution.py:36
  17.2 2.5 %collective-permute-start.23 = (bf16[64,3072]{1,0:T(8,128)(2,1)S(1)}, bf16[64,3072]{1,0:T(8,128)(2,1)S(1)}, u32[]{:S(2)}, u32[]{:S(2)}) collective-permute-start(bf16[64,3072]{1,0:T(8,128)(2,1)S(1)} %pad_maximum_fusion.3.refs_1_), channel_id=1, source_target_pairs={{0,6},{1,7},{2,0},{3,1},{4,2},{5,3},{6,4},{7,5},{8,14},{9,15},{10,... | collective-permute-start | bytes 1179656 | tf_op jit(solution)/shard_map/ppermute | solution.py:36
  19.8 1.8 %collective-permute-start.28 = (bf16[64,3072]{1,0:T(8,128)(2,1)S(1)}, bf16[64,3072]{1,0:T(8,128)(2,1)S(1)}, u32[]{:S(2)}, u32[]{:S(2)}) collective-permute-start(bf16[64,3072]{1,0:T(8,128)(2,1)S(1)} %pad_maximum_fusion.3.refs_1_), channel_id=1, source_target_pairs={{0,1},{1,0},{2,3},{3,2},{4,5},{5,4},{6,7},{7,6},{8,9},{9,8},{10,11... | collective-permute-start | bytes 1179656 | tf_op jit(solution)/shard_map/ppermute | solution.py:36
  23.3 1.8 %collective-permute-start.2 = (bf16[36,3072]{1,0:T(8,128)(2,1)S(1)}, bf16[36,3072]{1,0:T(8,128)(2,1)S(1)}, u32[]{:S(2)}, u32[]{:S(2)}) collective-permute-start(bf16[36,3072]{1,0:T(8,128)(2,1)S(1)} %get-tuple-element.18), channel_id=1, source_target_pairs={{0,24},{1,25},{2,26},{3,27},{4,28},{5,29},{6,30},{7,31},{8,0},{9,1... | collective-permute-start | bytes 663560 | tf_op jit(solution)/shard_map/ppermute | solution.py:36
  25.4 1.5 %collective-permute-start.1 = (bf16[36,3072]{1,0:T(8,128)(2,1)S(1)}, bf16[36,3072]{1,0:T(8,128)(2,1)S(1)}, u32[]{:S(2)}, u32[]{:S(2)}) collective-permute-start(bf16[36,3072]{1,0:T(8,128)(2,1)S(1)} %get-tuple-element.17), channel_id=1, source_target_pairs={{0,8},{1,9},{2,10},{3,11},{4,12},{5,13},{6,14},{7,15},{8,16},{9,17... | collective-permute-start | bytes 663560 | tf_op jit(solution)/shard_map/ppermute | solution.py:36
  27.5 2.3 %collective-permute-done.29.refs_5_ = bf16[64,3072]{1,0:T(8,128)(2,1)S(1)} collective-permute-done((bf16[64,3072]{1,0:T(8,128)(2,1)S(1)}, bf16[64,3072]{1,0:T(8,128)(2,1)S(1)}, u32[]{:S(2)}, u32[]{:S(2)}) %collective-permute-start.29) | collective-permute-done | bytes 393248 | tf_op jit(solution)/shard_map/ppermute | solution.py:36
  29.8 2.7 %collective-permute-start.32 = (bf16[80,3072]{1,0:T(8,128)(2,1)S(1)}, bf16[80,3072]{1,0:T(8,128)(2,1)S(1)}, u32[]{:S(2)}, u32[]{:S(2)}) collective-permute-start(bf16[80,3072]{1,0:T(8,128)(2,1)S(1)} %pad_maximum_fusion.1.refs_0_), channel_id=1, source_target_pairs={{0,6},{1,7},{2,0},{3,1},{4,2},{5,3},{6,4},{7,5},{8,14},{9,15},{10,... | collective-permute-start | bytes 1474568 | tf_op jit(solution)/shard_map/ppermute | solution.py:36
  32.5 5.8 %collective-permute-start.27 = (bf16[80,3072]{1,0:T(8,128)(2,1)S(1)}, bf16[80,3072]{1,0:T(8,128)(2,1)S(1)}, u32[]{:S(2)}, u32[]{:S(2)}) collective-permute-start(bf16[80,3072]{1,0:T(8,128)(2,1)S(1)} %pad_maximum_fusion.1.refs_0_), channel_id=1, source_target_pairs={{0,1},{1,0},{2,3},{3,2},{4,5},{5,4},{6,7},{7,6},{8,9},{9,8},{10,11... | collective-permute-start | bytes 1474568 | tf_op jit(solution)/shard_map/ppermute | solution.py:36
  39.0 2.0 %collective-permute-done.20.refs_4_ = bf16[80,3072]{1,0:T(8,128)(2,1)S(1)} collective-permute-done((bf16[80,3072]{1,0:T(8,128)(2,1)S(1)}, bf16[80,3072]{1,0:T(8,128)(2,1)S(1)}, u32[]{:S(2)}, u32[]{:S(2)}) %collective-permute-start.20) | collective-permute-done | bytes 491552 | tf_op jit(solution)/shard_map/ppermute | solution.py:36
  42.4 2.3 %collective-permute-start.24 = (bf16[64,3072]{1,0:T(8,128)(2,1)S(1)}, bf16[64,3072]{1,0:T(8,128)(2,1)S(1)}, u32[]{:S(2)}, u32[]{:S(2)}) collective-permute-start(bf16[64,3072]{1,0:T(8,128)(2,1)S(1)} %collective-permute-done.23.refs_9_), channel_id=1, source_target_pairs={{0,6},{1,7},{2,0},{3,1},{4,2},{5,3},{6,4},{7,5},{8,14},{9,15},{10,... | collective-permute-start | bytes 1179656 | tf_op jit(solution)/shard_map/ppermute | solution.py:36
  45.0 13.2 %collective-permute-done.24.refs_1_ = bf16[64,3072]{1,0:T(8,128)(2,1)S(1)} collective-permute-done((bf16[64,3072]{1,0:T(8,128)(2,1)S(1)}, bf16[64,3072]{1,0:T(8,128)(2,1)S(1)}, u32[]{:S(2)}, u32[]{:S(2)}) %collective-permute-start.24) | collective-permute-done | bytes 393248 | tf_op jit(solution)/shard_map/ppermute | solution.py:36
  58.2 2.7 %collective-permute-start.11 = (bf16[64,3072]{1,0:T(8,128)(2,1)S(1)}, bf16[64,3072]{1,0:T(8,128)(2,1)S(1)}, u32[]{:S(2)}, u32[]{:S(2)}) collective-permute-start(bf16[64,3072]{1,0:T(8,128)(2,1)S(1)} %pad_maximum_fusion.2.refs_1_), channel_id=1, source_target_pairs={{0,1},{1,0},{2,3},{3,2},{4,5},{5,4},{6,7},{7,6},{8,9},{9,8},{10,11... | collective-permute-start | bytes 1179656 | tf_op jit(solution)/shard_map/ppermute | solution.py:36
  60.9 3.3 %collective-permute-start.15 = (bf16[80,3072]{1,0:T(8,128)(2,1)S(1)}, bf16[80,3072]{1,0:T(8,128)(2,1)S(1)}, u32[]{:S(2)}, u32[]{:S(2)}) collective-permute-start(bf16[80,3072]{1,0:T(8,128)(2,1)S(1)} %pad_maximum_fusion.refs_0_), channel_id=1, source_target_pairs={{0,6},{1,7},{2,0},{3,1},{4,2},{5,3},{6,4},{7,5},{8,14},{9,15},{10,... | collective-permute-start | bytes 1474568 | tf_op jit(solution)/shard_map/ppermute | solution.py:36
  64.7 4.4 %collective-permute-start.33 = (bf16[80,3072]{1,0:T(8,128)(2,1)S(1)}, bf16[80,3072]{1,0:T(8,128)(2,1)S(1)}, u32[]{:S(2)}, u32[]{:S(2)}) collective-permute-start(bf16[80,3072]{1,0:T(8,128)(2,1)S(1)} %collective-permute-done.32.refs_8_), channel_id=1, source_target_pairs={{0,1},{1,0},{2,3},{3,2},{4,5},{5,4},{6,7},{7,6},{8,9},{9,8},{10,11... | collective-permute-start | bytes 1474568 | tf_op jit(solution)/shard_map/ppermute | solution.py:36
  69.1 2.5 %collective-permute-done.21.refs_0_ = bf16[80,3072]{1,0:T(8,128)(2,1)S(1)} collective-permute-done((bf16[80,3072]{1,0:T(8,128)(2,1)S(1)}, bf16[80,3072]{1,0:T(8,128)(2,1)S(1)}, u32[]{:S(2)}, u32[]{:S(2)}) %collective-permute-start.21) | collective-permute-done | bytes 491552 | tf_op jit(solution)/shard_map/ppermute | solution.py:36
  71.6 4.2 %collective-permute-start.25 = (bf16[80,3072]{1,0:T(8,128)(2,1)S(1)}, bf16[80,3072]{1,0:T(8,128)(2,1)S(1)}, u32[]{:S(2)}, u32[]{:S(2)}) collective-permute-start(bf16[80,3072]{1,0:T(8,128)(2,1)S(1)} %collective-permute-done.21.refs_0_), channel_id=1, source_target_pairs={{0,1},{1,0},{2,3},{3,2},{4,5},{5,4},{6,7},{7,6},{8,9},{9,8},{10,11... | collective-permute-start | bytes 1474568 | tf_op jit(solution)/shard_map/ppermute | solution.py:36
  78.3 1.4 router.3
  79.6 2.7 %collective-permute-start.7 = (bf16[64,3072]{1,0:T(8,128)(2,1)S(1)}, bf16[64,3072]{1,0:T(8,128)(2,1)S(1)}, u32[]{:S(2)}, u32[]{:S(2)}) collective-permute-start(bf16[64,3072]{1,0:T(8,128)(2,1)S(1)} %collective-permute-done.6.refs_9_), channel_id=1, source_target_pairs={{0,6},{1,7},{2,0},{3,1},{4,2},{5,3},{6,4},{7,5},{8,14},{9,15},{10,... | collective-permute-start | bytes 1179656 | tf_op jit(solution)/shard_map/ppermute | solution.py:36
  84.0 18.2 %experts.4.refs_5_ = bf16[2,1152,1024]{2,1,0:T(8,128)(2,1)} custom-call(s32[2,2,2048]{2,1,0:T(2,128)S(1)} %bitcast.25, s32[8,864]{1,0:T(8,128)S(1)} %copy-done.13, bf16[80,3072]{1,0:T(8,128)(2,1)S(1)} %pad_maximum_fusion.1.refs_0_, bf16[64,3072]{1,0:T(8,128)(2,1)S(1)} %pad_maximum_fusion.3.refs_1_, bf16[80,3072]{1,0:T(8,128)(2,1)S(1)} %collective-permute-done.27.refs_2_, ...), custom_call_target="tpu_custom_call" | custom-call | flops 7474249728 | bytes 13959168 | tf_op jit(solution)/shard_map/experts/pallas_call | solution.py:211
  102.2 10.3 %experts.5.refs_13_ = bf16[2,1152,1024]{2,1,0:T(8,128)(2,1)} custom-call(s32[2,2,2048]{2,1,0:T(2,128)S(1)} %bitcast.26, s32[8,288]{1,0:T(8,128)S(1)} %copy-done.11, bf16[80,3072]{1,0:T(8,128)(2,1)S(1)} %collective-permute-done.21.refs_0_, bf16[64,3072]{1,0:T(8,128)(2,1)S(1)} %collective-permute-done.24.refs_1_, ...), custom_call_target="tpu_custom_call", output_to_operand_aliasing={{}: (7, {})} | custom-call | flops 2491416576 | bytes 12779520 | tf_op jit(solution)/shard_map/experts/pallas_call | solution.py:211
  113.2 18.2 %experts.6.refs_5_ = bf16[2,1152,1024]{2,1,0:T(8,128)(2,1)} custom-call(s32[2,2,2048]{2,1,0:T(2,128)S(1)} %bitcast.27, s32[8,864]{1,0:T(8,128)S(1)} %copy-done.13, bf16[80,3072]{1,0:T(8,128)(2,1)S(1)} %pad_maximum_fusion.refs_0_, bf16[64,3072]{1,0:T(8,128)(2,1)S(1)} %pad_maximum_fusion.2.refs_1_, ...), custom_call_target="tpu_custom_call", output_to_operand_aliasing={{}: (15, {})} | custom-call | flops 7474249728 | bytes 13959168 | tf_op jit(solution)/shard_map/experts/pallas_call | solution.py:211
  131.5 10.3 %experts.7 = bf16[2,1152,1024]{2,1,0:T(8,128)(2,1)} custom-call(s32[2,2,2048]{2,1,0:T(2,128)S(1)} %bitcast.28, s32[8,288]{1,0:T(8,128)S(1)} %copy-done.11, bf16[80,3072]{1,0:T(8,128)(2,1)S(1)} %collective-permute-done.4.refs_0_, bf16[64,3072]{1,0:T(8,128)(2,1)S(1)} %collective-permute-done.7.refs_1_, ...), custom_call_target="tpu_custom_call", output_to_operand_aliasing={{}: (7, {})} | custom-call | flops 2491416576 | bytes 12779520 | tf_op jit(solution)/shard_map/experts/pallas_call | solution.py:211
  (90 shorter events, 17.6 us)
Async XLA Ops:
  3.8 13.4 %collective-permute-start.19 = (bf16[36,3072]{1,0:T(8,128)(2,1)S(1)}, bf16[36,3072]{1,0:T(8,128)(2,1)S(1)}, u32[]{:S(2)}, u32[]{:S(2)}) collective-permute-start(bf16[36,3072]{1,0:T(8,128)(2,1)S(1)} %get-tuple-element.22), channel_id=1, source_target_pairs={{0,24},{1,25},{2,26},{3,27},{4,28},{5,29},{6,30},{7,31},{8,0},{9,1... | collective-permute-start | bytes 663560 | tf_op jit(solution)/shard_map/ppermute | solution.py:36
  4.3 12.9 %collective-permute-start.22 = (bf16[36,3072]{1,0:T(8,128)(2,1)S(1)}, bf16[36,3072]{1,0:T(8,128)(2,1)S(1)}, u32[]{:S(2)}, u32[]{:S(2)}) collective-permute-start(bf16[36,3072]{1,0:T(8,128)(2,1)S(1)} %get-tuple-element.23), channel_id=1, source_target_pairs={{0,16},{1,17},{2,18},{3,19},{4,20},{5,21},{6,22},{7,23},{8,24},{9,... | collective-permute-start | bytes 663560 | tf_op jit(solution)/shard_map/ppermute | solution.py:36
  9.6 12.0 %collective-permute-start = (bf16[64,3072]{1,0:T(8,128)(2,1)S(1)}, bf16[64,3072]{1,0:T(8,128)(2,1)S(1)}, u32[]{:S(2)}, u32[]{:S(2)}) collective-permute-start(bf16[64,3072]{1,0:T(8,128)(2,1)S(1)} %get-tuple-element.13), channel_id=1, source_target_pairs={{32,0},{64,32},{96,64},{128,96},{160,128},{192,160},{224,192},{33,... | collective-permute-start | bytes 1179656 | tf_op jit(solution)/shard_map/ppermute | solution.py:41
  25.4 12.9 %collective-permute-start.1 = (bf16[36,3072]{1,0:T(8,128)(2,1)S(1)}, bf16[36,3072]{1,0:T(8,128)(2,1)S(1)}, u32[]{:S(2)}, u32[]{:S(2)}) collective-permute-start(bf16[36,3072]{1,0:T(8,128)(2,1)S(1)} %get-tuple-element.17), channel_id=1, source_target_pairs={{0,8},{1,9},{2,10},{3,11},{4,12},{5,13},{6,14},{7,15},{8,16},{9,17... | collective-permute-start | bytes 663560 | tf_op jit(solution)/shard_map/ppermute | solution.py:36
  26.9 11.5 %collective-permute-start.5 = (bf16[36,3072]{1,0:T(8,128)(2,1)S(1)}, bf16[36,3072]{1,0:T(8,128)(2,1)S(1)}, u32[]{:S(2)}, u32[]{:S(2)}) collective-permute-start(bf16[36,3072]{1,0:T(8,128)(2,1)S(1)} %get-tuple-element.19), channel_id=1, source_target_pairs={{0,16},{1,17},{2,18},{3,19},{4,20},{5,21},{6,22},{7,23},{8,24},{9,... | collective-permute-start | bytes 663560 | tf_op jit(solution)/shard_map/ppermute | solution.py:36
  29.8 11.2 %collective-permute-start.20 = (bf16[80,3072]{1,0:T(8,128)(2,1)S(1)}, bf16[80,3072]{1,0:T(8,128)(2,1)S(1)}, u32[]{:S(2)}, u32[]{:S(2)}) collective-permute-start(bf16[80,3072]{1,0:T(8,128)(2,1)S(1)} %pad_maximum_fusion.1.refs_0_), channel_id=1, source_target_pairs={{0,2},{1,3},{2,4},{3,5},{4,6},{5,7},{6,0},{7,1},{8,10},{9,11},{10,... | collective-permute-start | bytes 1474568 | tf_op jit(solution)/shard_map/ppermute | solution.py:36
  29.8 12.2 %collective-permute-start.32 = (bf16[80,3072]{1,0:T(8,128)(2,1)S(1)}, bf16[80,3072]{1,0:T(8,128)(2,1)S(1)}, u32[]{:S(2)}, u32[]{:S(2)}) collective-permute-start(bf16[80,3072]{1,0:T(8,128)(2,1)S(1)} %pad_maximum_fusion.1.refs_0_), channel_id=1, source_target_pairs={{0,6},{1,7},{2,0},{3,1},{4,2},{5,3},{6,4},{7,5},{8,14},{9,15},{10,... | collective-permute-start | bytes 1474568 | tf_op jit(solution)/shard_map/ppermute | solution.py:36
  41.0 20.0 %collective-permute-start.6 = (bf16[64,3072]{1,0:T(8,128)(2,1)S(1)}, bf16[64,3072]{1,0:T(8,128)(2,1)S(1)}, u32[]{:S(2)}, u32[]{:S(2)}) collective-permute-start(bf16[64,3072]{1,0:T(8,128)(2,1)S(1)} %pad_maximum_fusion.2.refs_1_), channel_id=1, source_target_pairs={{0,6},{1,7},{2,0},{3,1},{4,2},{5,3},{6,4},{7,5},{8,14},{9,15},{10,... | collective-permute-start | bytes 1179656 | tf_op jit(solution)/shard_map/ppermute | solution.py:36
  42.0 22.2 %collective-permute-start.12 = (bf16[64,3072]{1,0:T(8,128)(2,1)S(1)}, bf16[64,3072]{1,0:T(8,128)(2,1)S(1)}, u32[]{:S(2)}, u32[]{:S(2)}) collective-permute-start(bf16[64,3072]{1,0:T(8,128)(2,1)S(1)} %pad_maximum_fusion.2.refs_1_), channel_id=1, source_target_pairs={{0,2},{1,3},{2,4},{3,5},{4,6},{5,7},{6,0},{7,1},{8,10},{9,11},{10,... | collective-permute-start | bytes 1179656 | tf_op jit(solution)/shard_map/ppermute | solution.py:36
  42.4 15.8 %collective-permute-start.24 = (bf16[64,3072]{1,0:T(8,128)(2,1)S(1)}, bf16[64,3072]{1,0:T(8,128)(2,1)S(1)}, u32[]{:S(2)}, u32[]{:S(2)}) collective-permute-start(bf16[64,3072]{1,0:T(8,128)(2,1)S(1)} %collective-permute-done.23.refs_9_), channel_id=1, source_target_pairs={{0,6},{1,7},{2,0},{3,1},{4,2},{5,3},{6,4},{7,5},{8,14},{9,15},{10,... | collective-permute-start | bytes 1179656 | tf_op jit(solution)/shard_map/ppermute | solution.py:36
  44.8 19.9 %collective-permute-start.3 = (bf16[80,3072]{1,0:T(8,128)(2,1)S(1)}, bf16[80,3072]{1,0:T(8,128)(2,1)S(1)}, u32[]{:S(2)}, u32[]{:S(2)}) collective-permute-start(bf16[80,3072]{1,0:T(8,128)(2,1)S(1)} %pad_maximum_fusion.refs_0_), channel_id=1, source_target_pairs={{0,2},{1,3},{2,4},{3,5},{4,6},{5,7},{6,0},{7,1},{8,10},{9,11},{10,... | collective-permute-start | bytes 1474568 | tf_op jit(solution)/shard_map/ppermute | solution.py:36
  44.9 26.7 %collective-permute-start.21 = (bf16[80,3072]{1,0:T(8,128)(2,1)S(1)}, bf16[80,3072]{1,0:T(8,128)(2,1)S(1)}, u32[]{:S(2)}, u32[]{:S(2)}) collective-permute-start(bf16[80,3072]{1,0:T(8,128)(2,1)S(1)} %collective-permute-done.20.refs_4_), channel_id=1, source_target_pairs={{0,2},{1,3},{2,4},{3,5},{4,6},{5,7},{6,0},{7,1},{8,10},{9,11},{10,... | collective-permute-start | bytes 1474568 | tf_op jit(solution)/shard_map/ppermute | solution.py:36
  60.9 14.9 %collective-permute-start.15 = (bf16[80,3072]{1,0:T(8,128)(2,1)S(1)}, bf16[80,3072]{1,0:T(8,128)(2,1)S(1)}, u32[]{:S(2)}, u32[]{:S(2)}) collective-permute-start(bf16[80,3072]{1,0:T(8,128)(2,1)S(1)} %pad_maximum_fusion.refs_0_), channel_id=1, source_target_pairs={{0,6},{1,7},{2,0},{3,1},{4,2},{5,3},{6,4},{7,5},{8,14},{9,15},{10,... | collective-permute-start | bytes 1474568 | tf_op jit(solution)/shard_map/ppermute | solution.py:36
  64.2 11.6 %collective-permute-start.10 = (bf16[80,3072]{1,0:T(8,128)(2,1)S(1)}, bf16[80,3072]{1,0:T(8,128)(2,1)S(1)}, u32[]{:S(2)}, u32[]{:S(2)}) collective-permute-start(bf16[80,3072]{1,0:T(8,128)(2,1)S(1)} %pad_maximum_fusion.refs_0_), channel_id=1, source_target_pairs={{0,1},{1,0},{2,3},{3,2},{4,5},{5,4},{6,7},{7,6},{8,9},{9,8},{10,11... | collective-permute-start | bytes 1474568 | tf_op jit(solution)/shard_map/ppermute | solution.py:36
  64.5 15.2 %collective-permute-start.30 = (bf16[80,3072]{1,0:T(8,128)(2,1)S(1)}, bf16[80,3072]{1,0:T(8,128)(2,1)S(1)}, u32[]{:S(2)}, u32[]{:S(2)}) collective-permute-start(bf16[80,3072]{1,0:T(8,128)(2,1)S(1)} %collective-permute-done.20.refs_4_), channel_id=1, source_target_pairs={{0,1},{1,0},{2,3},{3,2},{4,5},{5,4},{6,7},{7,6},{8,9},{9,8},{10,11... | collective-permute-start | bytes 1474568 | tf_op jit(solution)/shard_map/ppermute | solution.py:36
  64.7 17.7 %collective-permute-start.33 = (bf16[80,3072]{1,0:T(8,128)(2,1)S(1)}, bf16[80,3072]{1,0:T(8,128)(2,1)S(1)}, u32[]{:S(2)}, u32[]{:S(2)}) collective-permute-start(bf16[80,3072]{1,0:T(8,128)(2,1)S(1)} %collective-permute-done.32.refs_8_), channel_id=1, source_target_pairs={{0,1},{1,0},{2,3},{3,2},{4,5},{5,4},{6,7},{7,6},{8,9},{9,8},{10,11... | collective-permute-start | bytes 1474568 | tf_op jit(solution)/shard_map/ppermute | solution.py:36
  71.6 11.6 %collective-permute-start.25 = (bf16[80,3072]{1,0:T(8,128)(2,1)S(1)}, bf16[80,3072]{1,0:T(8,128)(2,1)S(1)}, u32[]{:S(2)}, u32[]{:S(2)}) collective-permute-start(bf16[80,3072]{1,0:T(8,128)(2,1)S(1)} %collective-permute-done.21.refs_0_), channel_id=1, source_target_pairs={{0,1},{1,0},{2,3},{3,2},{4,5},{5,4},{6,7},{7,6},{8,9},{9,8},{10,11... | collective-permute-start | bytes 1474568 | tf_op jit(solution)/shard_map/ppermute | solution.py:36
  79.6 32.9 %collective-permute-start.7 = (bf16[64,3072]{1,0:T(8,128)(2,1)S(1)}, bf16[64,3072]{1,0:T(8,128)(2,1)S(1)}, u32[]{:S(2)}, u32[]{:S(2)}) collective-permute-start(bf16[64,3072]{1,0:T(8,128)(2,1)S(1)} %collective-permute-done.6.refs_9_), channel_id=1, source_target_pairs={{0,6},{1,7},{2,0},{3,1},{4,2},{5,3},{6,4},{7,5},{8,14},{9,15},{10,... | collective-permute-start | bytes 1179656 | tf_op jit(solution)/shard_map/ppermute | solution.py:36
  82.3 30.8 %collective-permute-start.14 = (bf16[64,3072]{1,0:T(8,128)(2,1)S(1)}, bf16[64,3072]{1,0:T(8,128)(2,1)S(1)}, u32[]{:S(2)}, u32[]{:S(2)}) collective-permute-start(bf16[64,3072]{1,0:T(8,128)(2,1)S(1)} %collective-permute-done.12.refs_5_), channel_id=1, source_target_pairs={{0,1},{1,0},{2,3},{3,2},{4,5},{5,4},{6,7},{7,6},{8,9},{9,8},{10,11... | collective-permute-start | bytes 1179656 | tf_op jit(solution)/shard_map/ppermute | solution.py:36
  83.1 30.0 %collective-permute-start.13 = (bf16[80,3072]{1,0:T(8,128)(2,1)S(1)}, bf16[80,3072]{1,0:T(8,128)(2,1)S(1)}, u32[]{:S(2)}, u32[]{:S(2)}) collective-permute-start(bf16[80,3072]{1,0:T(8,128)(2,1)S(1)} %collective-permute-done.3.refs_4_), channel_id=1, source_target_pairs={{0,1},{1,0},{2,3},{3,2},{4,5},{5,4},{6,7},{7,6},{8,9},{9,8},{10,11... | collective-permute-start | bytes 1474568 | tf_op jit(solution)/shard_map/ppermute | solution.py:36
  83.2 29.5 %collective-permute-start.4 = (bf16[80,3072]{1,0:T(8,128)(2,1)S(1)}, bf16[80,3072]{1,0:T(8,128)(2,1)S(1)}, u32[]{:S(2)}, u32[]{:S(2)}) collective-permute-start(bf16[80,3072]{1,0:T(8,128)(2,1)S(1)} %collective-permute-done.3.refs_4_), channel_id=1, source_target_pairs={{0,2},{1,3},{2,4},{3,5},{4,6},{5,7},{6,0},{7,1},{8,10},{9,11},{10,... | collective-permute-start | bytes 1474568 | tf_op jit(solution)/shard_map/ppermute | solution.py:36
  83.2 29.9 %collective-permute-start.16 = (bf16[80,3072]{1,0:T(8,128)(2,1)S(1)}, bf16[80,3072]{1,0:T(8,128)(2,1)S(1)}, u32[]{:S(2)}, u32[]{:S(2)}) collective-permute-start(bf16[80,3072]{1,0:T(8,128)(2,1)S(1)} %collective-permute-done.15.refs_8_), channel_id=1, source_target_pairs={{0,1},{1,0},{2,3},{3,2},{4,5},{5,4},{6,7},{7,6},{8,9},{9,8},{10,11... | collective-permute-start | bytes 1474568 | tf_op jit(solution)/shard_map/ppermute | solution.py:36
  112.6 18.9 %collective-permute-start.9 = (bf16[64,3072]{1,0:T(8,128)(2,1)S(1)}, bf16[64,3072]{1,0:T(8,128)(2,1)S(1)}, u32[]{:S(2)}, u32[]{:S(2)}) collective-permute-start(bf16[64,3072]{1,0:T(8,128)(2,1)S(1)} %collective-permute-done.7.refs_1_), channel_id=1, source_target_pairs={{0,1},{1,0},{2,3},{3,2},{4,5},{5,4},{6,7},{7,6},{8,9},{9,8},{10,11... | collective-permute-start | bytes 1179656 | tf_op jit(solution)/shard_map/ppermute | solution.py:36
  112.7 18.7 %collective-permute-start.8 = (bf16[80,3072]{1,0:T(8,128)(2,1)S(1)}, bf16[80,3072]{1,0:T(8,128)(2,1)S(1)}, u32[]{:S(2)}, u32[]{:S(2)}) collective-permute-start(bf16[80,3072]{1,0:T(8,128)(2,1)S(1)} %collective-permute-done.4.refs_0_), channel_id=1, source_target_pairs={{0,1},{1,0},{2,3},{3,2},{4,5},{5,4},{6,7},{7,6},{8,9},{9,8},{10,11... | collective-permute-start | bytes 1474568 | tf_op jit(solution)/shard_map/ppermute | solution.py:36
  (25 other events, 411.1 us)
where the time goes:
time: 145 us; the launch traced here: 142 us
  Pallas kernels  61 us (42%)
  starting transfers between devices  45.4 us (31%)
  waiting for transfers between devices  25.3 us (17%)
  local copies, waits for them, and re-layouts  8.83 us (6%)
    pallas_call x4, Pallas kernels, experts(): pl.pallas_call(functools.partial(experts_kernel, moment, sizes, earlier),...  57.1 us
    ppermute x34, starting transfers between devices, hop(): return lax.ppermute(shard, 'ep', pairs)  42.8 us
    ppermute x34, waiting for transfers between devices, hop(): return lax.ppermute(shard, 'ep', pairs)  25.3 us
    unnamed x28, local copies, waits for them, and re-layouts  8.79 us
  transfers between devices with their start and end apart: 35, of which 6 were waited for; matrix products, arithmetic and copies ran while one was open for 0% of the time, Pallas kernels for 35%

commit v1 on v0

v1 whole, which is shorter than its diff:
```python
import functools

import jax
import jax.numpy as jnp
import numpy as np
from jax import lax
from jax.experimental import pallas as pl
from jax.experimental.pallas import tpu as pltpu
from jax.sharding import PartitionSpec as P

TICKS = 2
CAP = 36
XS, YS, CORES = 4, 4, 2
EP = XS * YS * CORES
TOKENS = 64
D = 3072
HID = 1024
MAXP = EP * CAP
BLOCK = YS * CAP
HEAD = 80
DYS = (0, 1, 3, 2)
GROUP = CORES * BLOCK
STEP = 128
PLACED = 384
VMEM = pl.BlockSpec(memory_space=pltpu.VMEM)
ANY = pl.BlockSpec(memory_space=pl.ANY)
CHEAP = pl.CostEstimate(flops=1024, bytes_accessed=1024, transcendentals=0)
NT = (((1,), (1,)), ((), ()))


def hop(shard, dy=0, dx=0, dc=0):
    pairs = []
    for y in range(YS):
        for x in range(XS):
            for c in range(CORES):
                to = (((y + dy) % YS) * XS + (x + dx) % XS) * CORES + (c + dc) % CORES
                pairs.append(((y * XS + x) * CORES + c, to))
    return lax.ppermute(shard, "ep", pairs)


def down(shard):
    n = lax.axis_size("section")
    return lax.ppermute(shard, "section", [(i, i - 1) for i in range(1, n)])


def own_ids_of(ids_ref, moment, me):
    both = ids_ref[moment, :, pl.ds(pl.multiple_of((me // 2) * 128, 128), 128)].astype(jnp.float32)
    return jnp.where(me % 2 == 0, both[:, :TOKENS], both[:, TOKENS:])


def gradient_of(refs):
    if len(refs) == 1:
        return refs[0][...]
    top, moved = refs
    last = lax.axis_index("section") == lax.axis_size("section") - 1
    return jnp.where(last, top[...], moved[...])


def route_kernel(moment, ids_ref, share_ref, *refs):
    grads, outs = refs[:-YS], refs[-YS:]
    me = lax.axis_index("ep")
    my_y = (me // (XS * CORES)).astype(jnp.float32)
    own = own_ids_of(ids_ref, moment, me)
    first, second = own[0:1], own[1:2]
    experts = lax.broadcasted_iota(jnp.int32, (8, TOKENS), 0).astype(jnp.float32)
    is_first, is_second = experts == first, experts == second
    chosen = (is_first | is_second).astype(jnp.float32).astype(jnp.bfloat16)
    before = lax.broadcasted_iota(jnp.int32, (TOKENS, TOKENS), 0) < lax.broadcasted_iota(
        jnp.int32, (TOKENS, TOKENS), 1
    )
    ranks = jnp.dot(chosen, before.astype(jnp.float32).astype(jnp.bfloat16), preferred_element_type=jnp.float32)

    def place(expert, mask):
        relative = expert - my_y
        relative = jnp.where(relative < 0, relative + YS, relative)
        return relative * CAP + jnp.sum(jnp.where(mask, ranks, 0.0), 0, keepdims=True)

    place_1, place_2 = place(first, is_first), place(second, is_second)
    share = share_ref[moment : moment + 1, :]
    gradient = gradient_of(grads)
    slots = lax.broadcasted_iota(jnp.int32, (CAP, TOKENS), 0).astype(jnp.float32)
    for j in range(YS):
        one, two = slots + j * CAP == place_1, slots + j * CAP == place_2
        weight = jnp.sum(jnp.where(one, share, 0.0) + jnp.where(two, 1.0 - share, 0.0), 1, keepdims=True)
        placing = (one | two).astype(jnp.float32).astype(jnp.bfloat16)
        rows = jnp.dot(placing, gradient, preferred_element_type=jnp.float32)
        outs[j][...] = (rows * weight).astype(jnp.bfloat16)


def whole(array):
    rank = len(array.shape)
    return pl.BlockSpec(array.shape, lambda i: (0,) * rank)


def route(moment, ids, share, grads):
    return pl.pallas_call(
        functools.partial(route_kernel, moment),
        grid=(1,),
        out_shape=[jax.ShapeDtypeStruct((CAP, D), jnp.bfloat16)] * YS,
        in_specs=[whole(a) for a in (ids, share, *grads)],
        out_specs=[pl.BlockSpec((CAP, D), lambda i: (0, 0))] * YS,
        compiler_params=pltpu.CompilerParams(vmem_limit_bytes=16 << 20),
        cost_estimate=CHEAP,
        name="route",
    )(ids, share, *grads)


def router_kernel(moment, count, ids_ref, share_ref, router_ref, gap_ref, *refs):
    grads, outs = refs[:count], refs[-2:]
    me = lax.axis_index("ep")
    own = own_ids_of(ids_ref, moment, me)
    eye = lax.broadcasted_iota(jnp.int32, (TOKENS, TOKENS), 0) == lax.broadcasted_iota(
        jnp.int32, (TOKENS, TOKENS), 1
    )

    def upright(row):
        return jnp.sum(jnp.where(eye, row, 0.0), 1, keepdims=True)

    first, second = upright(own[0:1]), upright(own[1:2])
    share = upright(share_ref[moment : moment + 1, :])
    gradient = gradient_of(grads).astype(jnp.float32)
    gap_dot = jnp.sum(gradient * gap_ref[0].astype(jnp.float32), 1, keepdims=True)
    logit_grad = share * (1.0 - share) * gap_dot
    term = jnp.zeros((TOKENS, D), jnp.float32)
    for e in range(YS):
        sign = jnp.where(first == e, 1.0, 0.0) - jnp.where(second == e, 1.0, 0.0)
        term = term + (logit_grad * sign) * router_ref[e : e + 1, :]
    departing = (gradient + term).astype(jnp.bfloat16)
    outs[0][0] = departing
    outs[1][...] = departing


def router(moment, ids, share, router_rows, gap, grads, departs):
    more = [] if departs is None else [departs]
    return pl.pallas_call(
        functools.partial(router_kernel, moment, len(grads)),
        grid=(1,),
        out_shape=[
            jax.ShapeDtypeStruct((TICKS, TOKENS, D), jnp.bfloat16),
            jax.ShapeDtypeStruct((TOKENS, D), jnp.bfloat16),
        ],
        in_specs=[whole(a) for a in (ids, share, router_rows)]
        + [pl.BlockSpec((1, TOKENS, D), lambda i: (moment, 0, 0))]
        + [whole(a) for a in grads]
        + [ANY] * len(more),
        out_specs=[
            pl.BlockSpec((1, TOKENS, D), lambda i: (moment, 0, 0)),
            pl.BlockSpec((TOKENS, D), lambda i: (0, 0)),
        ],
        input_output_aliases={4 + len(grads): 0} if more else {},
        compiler_params=pltpu.CompilerParams(vmem_limit_bytes=16 << 20),
        cost_estimate=CHEAP,
        name="router",
    )(ids, share, router_rows, gap, *grads, *more)


def load_rows(pieces, rows_ref, sems):
    copies, begin = [], 0
    for i, piece in enumerate(pieces):
        size = piece.shape[0]
        copies.append((begin, pltpu.make_async_copy(piece, rows_ref.at[pl.ds(begin, size)], sems.at[i])))
        copies[i][1].start()
        begin += size
    return copies


def multiply(copies, rows_ref, down_ref, product_ref, base):
    for begin in range(0, rows_ref.shape[0], GROUP):
        for at, copy in copies:
            if begin <= at < begin + GROUP:
                copy.wait()
        product = lax.dot_general(
            rows_ref[pl.ds(begin, GROUP), :], down_ref[...], NT, preferred_element_type=jnp.float32
        )
        product_ref[pl.ds(base + begin, GROUP), :] = product.astype(jnp.bfloat16)


def near_kernel(count, down_ref, *refs):
    product_ref, rows_ref, sems = refs[count:]
    multiply(load_rows(refs[:count], rows_ref, sems), rows_ref, down_ref, product_ref, 0)


def near_product(pieces, down_rows):
    total = sum(p.shape[0] for p in pieces)
    return pl.pallas_call(
        functools.partial(near_kernel, len(pieces)),
        out_shape=jax.ShapeDtypeStruct((total, HID), jnp.bfloat16),
        in_specs=[VMEM] + [ANY] * len(pieces),
        out_specs=VMEM,
        scratch_shapes=[pltpu.VMEM((total, D), jnp.bfloat16), pltpu.SemaphoreType.DMA((len(pieces),))],
        compiler_params=pltpu.CompilerParams(vmem_limit_bytes=24 << 20),
        cost_estimate=CHEAP,
        name="near_product",
    )(down_rows, *pieces)


def place_kernel(moment, count, ids_ref, table_ref, down_ref, *refs):
    pieces, near_ref = refs[:count], refs[count]
    out_ref, rows_ref, placing_ref, product_ref, placed_ref, sems = refs[-6:]
    copies = load_rows(pieces, rows_ref, sems)
    base = MAXP - rows_ref.shape[0]
    back = pltpu.make_async_copy(near_ref, product_ref.at[pl.ds(0, base)], sems.at[count])
    back.start()
    me = lax.axis_index("ep")
    my_y, my_x, my_c = me // (XS * CORES), (me // CORES) % XS, me % CORES
    named = (ids_ref[moment] == my_y).astype(jnp.float32)
    named = jnp.broadcast_to(named[0:1] + named[1:2], (8, EP * TOKENS)).astype(jnp.bfloat16)
    owner = lax.broadcasted_iota(jnp.int32, (EP, EP * TOKENS), 1) // TOKENS
    owned = owner == lax.broadcasted_iota(jnp.int32, (EP, EP * TOKENS), 0)
    counts = lax.dot_general(
        named, owned.astype(jnp.float32).astype(jnp.bfloat16), NT, preferred_element_type=jnp.float32
    ).astype(jnp.bfloat16)
    table = table_ref[...]
    source = (
        ((my_y - table[0:1]) & (YS - 1)) * (XS * CORES)
        + ((my_x - table[1:2]) & (XS - 1)) * CORES
        + ((my_c - table[2:3]) & (CORES - 1))
    )
    slot = table[3:4].astype(jnp.float32)
    device = lax.broadcasted_iota(jnp.int32, (EP, MAXP), 0)
    ahead = (device < source).astype(jnp.float32).astype(jnp.bfloat16)
    itself = (device == source).astype(jnp.float32).astype(jnp.bfloat16)
    offset = jnp.dot(counts, ahead, preferred_element_type=jnp.float32)[0:1]
    amount = jnp.dot(counts, itself, preferred_element_type=jnp.float32)[0:1]
    target = jnp.where(slot < amount, offset + slot, -1.0).astype(jnp.int32)

    @pl.loop(0, MAXP // STEP)
    def _(k):
        at = pl.multiple_of(k * STEP, STEP)
        here = lax.broadcasted_iota(jnp.int32, (STEP, MAXP), 0) + at
        placing_ref[pl.ds(at, STEP), :] = (here == target).astype(jnp.float32).astype(jnp.bfloat16)

    multiply(copies, rows_ref, down_ref, product_ref, base)
    back.wait()
    stores = []
    for k in range(MAXP // PLACED):
        part = pl.ds(k * PLACED, PLACED)
        placed = jnp.dot(placing_ref[part, :], product_ref[...], preferred_element_type=jnp.float32)
        placed_ref[part, :] = placed.astype(jnp.bfloat16)
        stores.append(
            pltpu.make_async_copy(placed_ref.at[part], out_ref.at[moment, part], sems.at[count + 1 + k])
        )
        stores[k].start()
    for store in stores:
        store.wait()


def place(moment, ids, pieces, near, order, down_rows, hidden):
    columns = [(dy, dx, dc, slot) for dx, dc in order for dy in DYS for slot in range(CAP)]
    table = np.zeros((8, MAXP), np.int32)
    table[:4] = np.array(columns, np.int32).T
    more = [] if hidden is None else [hidden]
    return pl.pallas_call(
        functools.partial(place_kernel, moment, len(pieces)),
        out_shape=jax.ShapeDtypeStruct((TICKS, MAXP, HID), jnp.bfloat16),
        in_specs=[VMEM] * 3 + [ANY] * (len(pieces) + 1 + len(more)),
        out_specs=ANY,
        scratch_shapes=[
            pltpu.VMEM((sum(p.shape[0] for p in pieces), D), jnp.bfloat16),
            pltpu.VMEM((MAXP, MAXP), jnp.bfloat16),
            pltpu.VMEM((MAXP, HID), jnp.bfloat16),
            pltpu.VMEM((MAXP, HID), jnp.bfloat16),
            pltpu.SemaphoreType.DMA((len(pieces) + 1 + MAXP // PLACED,)),
        ],
        input_output_aliases={4 + len(pieces): 0} if more else {},
        compiler_params=pltpu.CompilerParams(vmem_limit_bytes=24 << 20),
        cost_estimate=CHEAP,
        name="place",
    )(ids, jnp.asarray(table), down_rows, *pieces, near, *more)


def spread(parts):
    return {j: hop(parts[j], dy=j) for j in (1, 3, 2)}


def joined(own, came):
    return jnp.concatenate([own, came[1], came[3], came[2]], 0)


def beside(block):
    return {dx: hop(block, dx=dx) for dx in (1, 3)}


def opposite(near):
    return hop(near[1][:HEAD], dx=1), hop(near[3][HEAD:], dx=3)


def swapped(tree):
    return jax.tree.map(lambda p: hop(p, dc=1), tree)


NEAR = ((0, 0), (0, 1), (1, 0), (1, 1), (3, 0), (3, 1))
FAR = ((2, 0), (2, 1))


def local(arriving, top_grad, expert_ids, first_share, out_gap, router_weight, down_weight):
    tie = lax.optimization_barrier
    ids = jnp.swapaxes(expert_ids[0], 1, 2)
    share, gap, router_rows, down_rows = first_share[0], out_gap[0], router_weight[0], down_weight[0]

    parts0 = route(0, ids, share, [arriving[0]])
    parts0, gradient = tie((parts0, arriving[0]))
    departs, departing = router(0, ids, share, router_rows, gap, [gradient], None)
    own0, came0, moved = tie((parts0[0], spread(parts0), down(departing)))

    block0 = joined(own0, came0)
    near0 = beside(block0)
    grads = [top_grad[0], moved]
    parts1 = route(1, ids, share, grads)
    own1, came1, block0, near0, grads = tie((parts1[0], spread(parts1), block0, near0, grads))

    block1 = joined(own1, came1)
    far0 = opposite(near0)
    near1 = beside(block1)
    mate0, mates0 = swapped(block0), swapped(near0)
    pieces = [block0, mate0, near0[1], mates0[1], near0[3], mates0[3]]
    product0 = near_product(pieces, down_rows)
    departs, _ = router(1, ids, share, router_rows, gap, grads, departs)
    far0, block1, near1, product0, departs = tie((far0, block1, near1, product0, departs))

    far1 = opposite(near1)
    mate = swapped(far0)
    mate1, mates1 = swapped(block1), swapped(near1)
    hidden = place(0, ids, [*far0, *mate], product0, NEAR + FAR, down_rows, None)
    far1, near1, block1, mate1, mates1, hidden = tie((far1, near1, block1, mate1, mates1, hidden))

    mate = swapped(far1)
    pieces = [block1, mate1, near1[1], mates1[1], near1[3], mates1[3]]
    product1 = near_product(pieces, down_rows)
    hidden = place(1, ids, [*far1, *mate], product1, NEAR + FAR, down_rows, hidden)
    return departs[None], hidden[None]


def solution(mesh):
    placed = (
        P("section", "ep", None),
        P(None, "ep", None),
        P("section", None, None, None),
        P("section", None, "ep"),
        P("section", None, "ep", None),
        P("section", None, None),
        P("section", "ep", None),
    )
    return jax.shard_map(
        local,
        mesh=mesh,
        in_specs=placed,
        out_specs=(P("section", None, "ep", None), P("section", None, "ep", None)),
        check_vma=False,
    )
```

time: 145 us -> 117 us (0.81); the launches traced: 142 us -> 116 us
  waiting for transfers between devices: 25.3 us -> 51.1 us
  Pallas kernels: 61 us -> 35.2 us
  starting transfers between devices: 45.4 us -> 23.2 us
  local copies, waits for them, and re-layouts: 8.83 us -> 5.5 us
    pallas_call x6, Pallas kernels: 58.4 us -> 32.6 us  [the longest x2 16.8 us: place(): pl.pallas_call(functools.partial(place_kernel, moment, len(pieces)), out_...]
    ppermute x34 -> x24, waiting for transfers between devices: 25.3 us -> 51.1 us  [hop(): return lax.ppermute(shard, 'ep', pairs)]
    ppermute x34 -> x24, starting transfers between devices: 42.8 us -> 20.6 us  [hop(): return lax.ppermute(shard, 'ep', pairs)]
    unnamed x28 -> x26, local copies, waits for them, and re-layouts: 8.79 us -> 5.38 us
  transfers between devices with their start and end apart: 35 -> 25, of which waited for: 6 -> 11; matrix products, arithmetic and copies ran while one was open for 0% -> 0% of each run, Pallas kernels for 35% -> 21%
where the time goes in v1:
time: 117 us; the launch traced here: 116 us
  waiting for transfers between devices  51.1 us (44%)
  Pallas kernels  35.2 us (30%)
  starting transfers between devices  23.2 us (20%)
  local copies, waits for them, and re-layouts  5.5 us (5%)
    ppermute x24, waiting for transfers between devices, hop(): return lax.ppermute(shard, 'ep', pairs)  51.1 us
    ppermute x24, starting transfers between devices, hop(): return lax.ppermute(shard, 'ep', pairs)  20.6 us
    pallas_call x2, Pallas kernels, place(): pl.pallas_call(functools.partial(place_kernel, moment, len(pieces)), out_...  16.8 us
    pallas_call x2, Pallas kernels, near_product(): pl.pallas_call(functools.partial(near_kernel, len(pieces)), out_shape=jax...  14.4 us
    unnamed x26, local copies, waits for them, and re-layouts  5.38 us
    ppermute x1, starting transfers between devices, down(): return lax.ppermute(shard, 'section', [(i, i - 1) for i in range(1, n)])  2.64 us
    pallas_call x2, Pallas kernels, router(): pl.pallas_call(functools.partial(router_kernel, moment, len(grads)), grid...  2.6 us
  transfers between devices with their start and end apart: 25, of which 11 were waited for; matrix products, arithmetic and copies ran while one was open for 0% of the time, Pallas kernels for 21%

profile of v1, /device:TPU:249, one launch (start us, length us, event | category | flops | bytes accessed | tf_op | source)
XLA Modules:
  0.0 116.4 jit_solution(14325935675770631966)
XLA Ops:
  7.9 2.6 %collective-permute-start.3 = (bf16[64,3072]{1,0:T(8,128)(2,1)S(1)}, bf16[64,3072]{1,0:T(8,128)(2,1)S(1)}, u32[]{:S(2)}, u32[]{:S(2)}) collective-permute-start(bf16[64,3072]{1,0:T(8,128)(2,1)S(1)} %get-tuple-element.57), channel_id=1, source_target_pairs={{32,0},{64,32},{96,64},{128,96},{160,128},{192,160},{224,192},{33,... | collective-permute-start | bytes 1179656 | tf_op jit(solution)/shard_map/ppermute | solution.py:43
  10.6 2.2 %collective-permute-start.1 = (bf16[36,3072]{1,0:T(8,128)(2,1)S(1)}, bf16[36,3072]{1,0:T(8,128)(2,1)S(1)}, u32[]{:S(2)}, u32[]{:S(2)}) collective-permute-start(bf16[36,3072]{1,0:T(8,128)(2,1)S(1)} %get-tuple-element.54), channel_id=1, source_target_pairs={{0,16},{1,17},{2,18},{3,19},{4,20},{5,21},{6,22},{7,23},{8,24},{9,... | collective-permute-start | bytes 663560 | tf_op jit(solution)/shard_map/ppermute | solution.py:38
  12.9 4.2 %collective-permute-done = bf16[36,3072]{1,0:T(8,128)(2,1)S(1)} collective-permute-done((bf16[36,3072]{1,0:T(8,128)(2,1)S(1)}, bf16[36,3072]{1,0:T(8,128)(2,1)S(1)}, u32[]{:S(2)}, u32[]{:S(2)}) %collective-permute-start) | collective-permute-done | bytes 221216 | tf_op jit(solution)/shard_map/ppermute | solution.py:38
  17.1 1.5 %collective-permute-done.1 = bf16[36,3072]{1,0:T(8,128)(2,1)S(1)} collective-permute-done((bf16[36,3072]{1,0:T(8,128)(2,1)S(1)}, bf16[36,3072]{1,0:T(8,128)(2,1)S(1)}, u32[]{:S(2)}, u32[]{:S(2)}) %collective-permute-start.1) | collective-permute-done | bytes 221216 | tf_op jit(solution)/shard_map/ppermute | solution.py:38
  18.6 6.7 %collective-permute-done.2 = bf16[36,3072]{1,0:T(8,128)(2,1)S(1)} collective-permute-done((bf16[36,3072]{1,0:T(8,128)(2,1)S(1)}, bf16[36,3072]{1,0:T(8,128)(2,1)S(1)}, u32[]{:S(2)}, u32[]{:S(2)}) %collective-permute-start.2) | collective-permute-done | bytes 221216 | tf_op jit(solution)/shard_map/ppermute | solution.py:38
  25.5 1.3 %collective-permute-start.7 = (bf16[144,3072]{1,0:T(8,128)(2,1)S(1)}, bf16[144,3072]{1,0:T(8,128)(2,1)S(1)}, u32[]{:S(2)}, u32[]{:S(2)}) collective-permute-start(bf16[144,3072]{1,0:T(8,128)(2,1)S(1)} %pad_maximum_fusion.refs_0_), channel_id=1, source_target_pairs={{0,2},{1,3},{2,4},{3,5},{4,6},{5,7},{6,0},{7,1},{8,10},{9,11},{10,... | collective-permute-start | bytes 2654216 | tf_op jit(solution)/shard_map/ppermute | solution.py:38
  26.8 1.5 %collective-permute-start.8 = (bf16[144,3072]{1,0:T(8,128)(2,1)S(1)}, bf16[144,3072]{1,0:T(8,128)(2,1)S(1)}, u32[]{:S(2)}, u32[]{:S(2)}) collective-permute-start(bf16[144,3072]{1,0:T(8,128)(2,1)S(1)} %pad_maximum_fusion.refs_0_), channel_id=1, source_target_pairs={{0,6},{1,7},{2,0},{3,1},{4,2},{5,3},{6,4},{7,5},{8,14},{9,15},{10,... | collective-permute-start | bytes 2654216 | tf_op jit(solution)/shard_map/ppermute | solution.py:38
  30.7 4.8 %collective-permute-done.4 = bf16[36,3072]{1,0:T(8,128)(2,1)S(1)} collective-permute-done((bf16[36,3072]{1,0:T(8,128)(2,1)S(1)}, bf16[36,3072]{1,0:T(8,128)(2,1)S(1)}, u32[]{:S(2)}, u32[]{:S(2)}) %collective-permute-start.4) | collective-permute-done | bytes 221216 | tf_op jit(solution)/shard_map/ppermute | solution.py:38
  36.1 7.0 %collective-permute-done.6 = bf16[36,3072]{1,0:T(8,128)(2,1)S(1)} collective-permute-done((bf16[36,3072]{1,0:T(8,128)(2,1)S(1)}, bf16[36,3072]{1,0:T(8,128)(2,1)S(1)}, u32[]{:S(2)}, u32[]{:S(2)}) %collective-permute-start.6) | collective-permute-done | bytes 221216 | tf_op jit(solution)/shard_map/ppermute | solution.py:38
  43.1 4.5 %collective-permute-done.7.refs_2_ = bf16[144,3072]{1,0:T(8,128)(2,1)S(1)} collective-permute-done((bf16[144,3072]{1,0:T(8,128)(2,1)S(1)}, bf16[144,3072]{1,0:T(8,128)(2,1)S(1)}, u32[]{:S(2)}, u32[]{:S(2)}) %collective-permute-start.7) | collective-permute-done | bytes 884768 | tf_op jit(solution)/shard_map/ppermute | solution.py:38
  47.5 1.4 %collective-permute-start.13 = (bf16[144,3072]{1,0:T(8,128)(2,1)S(1)}, bf16[144,3072]{1,0:T(8,128)(2,1)S(1)}, u32[]{:S(2)}, u32[]{:S(2)}) collective-permute-start(bf16[144,3072]{1,0:T(8,128)(2,1)S(1)} %pad_maximum_fusion.refs_0_), channel_id=1, source_target_pairs={{0,1},{1,0},{2,3},{3,2},{4,5},{5,4},{6,7},{7,6},{8,9},{9,8},{10,11... | collective-permute-start | bytes 2654216 | tf_op jit(solution)/shard_map/ppermute | solution.py:38
  49.6 1.3 %collective-permute-start.11 = (bf16[144,3072]{1,0:T(8,128)(2,1)S(1)}, bf16[144,3072]{1,0:T(8,128)(2,1)S(1)}, u32[]{:S(2)}, u32[]{:S(2)}) collective-permute-start(bf16[144,3072]{1,0:T(8,128)(2,1)S(1)} %pad_maximum_fusion.1.refs_0_), channel_id=1, source_target_pairs={{0,2},{1,3},{2,4},{3,5},{4,6},{5,7},{6,0},{7,1},{8,10},{9,11},{10,... | collective-permute-start | bytes 2654216 | tf_op jit(solution)/shard_map/ppermute | solution.py:38
  50.9 1.6 %collective-permute-start.12 = (bf16[144,3072]{1,0:T(8,128)(2,1)S(1)}, bf16[144,3072]{1,0:T(8,128)(2,1)S(1)}, u32[]{:S(2)}, u32[]{:S(2)}) collective-permute-start(bf16[144,3072]{1,0:T(8,128)(2,1)S(1)} %pad_maximum_fusion.1.refs_0_), channel_id=1, source_target_pairs={{0,6},{1,7},{2,0},{3,1},{4,2},{5,3},{6,4},{7,5},{8,14},{9,15},{10,... | collective-permute-start | bytes 2654216 | tf_op jit(solution)/shard_map/ppermute | solution.py:38
  52.6 2.9 %collective-permute-start.10 = (bf16[64,3072]{1,0:T(8,128)(2,1)S(1)}, bf16[64,3072]{1,0:T(8,128)(2,1)S(1)}, u32[]{:S(2)}, u32[]{:S(2)}) collective-permute-start(bf16[64,3072]{1,0:T(8,128)(2,1)S(1)} %slice.13), channel_id=1, source_target_pairs={{0,6},{1,7},{2,0},{3,1},{4,2},{5,3},{6,4},{7,5},{8,14},{9,15},{10,... | collective-permute-start | bytes 1179656 | tf_op jit(solution)/shard_map/ppermute | solution.py:38
  55.5 1.4 %router.3 = (bf16[2,64,3072]{2,1,0:T(8,128)(2,1)}, bf16[64,3072]{1,0:T(8,128)(2,1)}) custom-call(s32[2,2,2048]{2,1,0:T(2,128)S(1)} %bitcast.24, f32[2,64]{1,0:T(2,128)S(1)} %bitcast.32, f32[4,3072]{1,0:T(4,128)S(1)} %bitcast.28, bf16[2,64,3072]{2,1,0:T(8,128)(2,1)S(1)} %bitcast.16, bf16[64,3072]{1,0:T(8,128)(2,1)S(1)} %bitcast.20, ...), custom_call_target="tpu_custom_call", output_to_operand_aliasing={{0}: (6, {})} | custom-call | flops 1024 | bytes 1024 | tf_op jit(solution)/shard_map/router/pallas_call | solution.py:135
  56.9 7.2 %near_product.2.refs_4_ = bf16[864,1024]{1,0:T(8,128)(2,1)S(1)} custom-call(bf16[1024,3072]{1,0:T(8,128)(2,1)S(1)} %bitcast.11, bf16[144,3072]{1,0:T(8,128)(2,1)S(1)} %pad_maximum_fusion.refs_0_, bf16[144,3072]{1,0:T(8,128)(2,1)S(1)} %collective-permute-done.13.refs_1_, bf16[144,3072]{1,0:T(8,128)(2,1)S(1)} %collective-permute-done.7.refs_2_, ...), custom_call_target="tpu_custom_call" | custom-call | flops 1024 | bytes 1024 | tf_op jit(solution)/shard_map/near_product/pallas_call | solution.py:185
  64.1 16.1 %collective-permute-done.10.refs_1_ = bf16[64,3072]{1,0:T(8,128)(2,1)S(1)} collective-permute-done((bf16[64,3072]{1,0:T(8,128)(2,1)S(1)}, bf16[64,3072]{1,0:T(8,128)(2,1)S(1)}, u32[]{:S(2)}, u32[]{:S(2)}) %collective-permute-start.10) | collective-permute-done | bytes 393248 | tf_op jit(solution)/shard_map/ppermute | solution.py:38
  80.2 2.4 %collective-permute-done.9.refs_0_ = bf16[80,3072]{1,0:T(8,128)(2,1)S(1)} collective-permute-done((bf16[80,3072]{1,0:T(8,128)(2,1)S(1)}, bf16[80,3072]{1,0:T(8,128)(2,1)S(1)}, u32[]{:S(2)}, u32[]{:S(2)}) %collective-permute-start.9) | collective-permute-done | bytes 491552 | tf_op jit(solution)/shard_map/ppermute | solution.py:38
  85.6 3.0 %collective-permute-start.17 = (bf16[64,3072]{1,0:T(8,128)(2,1)S(1)}, bf16[64,3072]{1,0:T(8,128)(2,1)S(1)}, u32[]{:S(2)}, u32[]{:S(2)}) collective-permute-start(bf16[64,3072]{1,0:T(8,128)(2,1)S(1)} %slice.15), channel_id=1, source_target_pairs={{0,6},{1,7},{2,0},{3,1},{4,2},{5,3},{6,4},{7,5},{8,14},{9,15},{10,... | collective-permute-start | bytes 1179656 | tf_op jit(solution)/shard_map/ppermute | solution.py:38
  88.5 8.4 %place.2.refs_5_ = bf16[2,1152,1024]{2,1,0:T(8,128)(2,1)} custom-call(s32[2,2,2048]{2,1,0:T(2,128)S(1)} %bitcast.25, s32[8,1152]{1,0:T(8,128)S(1)} %copy-done.10, bf16[1024,3072]{1,0:T(8,128)(2,1)S(1)} %bitcast.12, bf16[80,3072]{1,0:T(8,128)(2,1)S(1)} %collective-permute-done.9.refs_0_, bf16[64,3072]{1,0:T(8,128)(2,1)S(1)} %collective-permute-done.10.refs_1_, ...), custom_call_target="tpu_custom_call" | custom-call | flops 1024 | bytes 1024 | tf_op jit(solution)/shard_map/place/pallas_call | solution.py:253
  97.0 2.2 %collective-permute-done.16.refs_0_ = bf16[80,3072]{1,0:T(8,128)(2,1)S(1)} collective-permute-done((bf16[80,3072]{1,0:T(8,128)(2,1)S(1)}, bf16[80,3072]{1,0:T(8,128)(2,1)S(1)}, u32[]{:S(2)}, u32[]{:S(2)}) %collective-permute-start.16) | collective-permute-done | bytes 491552 | tf_op jit(solution)/shard_map/ppermute | solution.py:38
  99.2 1.3 %collective-permute-start.23 = (bf16[80,3072]{1,0:T(8,128)(2,1)S(1)}, bf16[80,3072]{1,0:T(8,128)(2,1)S(1)}, u32[]{:S(2)}, u32[]{:S(2)}) collective-permute-start(bf16[80,3072]{1,0:T(8,128)(2,1)S(1)} %collective-permute-done.16.refs_0_), channel_id=1, source_target_pairs={{0,1},{1,0},{2,3},{3,2},{4,5},{5,4},{6,7},{7,6},{8,9},{9,8},{10,11... | collective-permute-start | bytes 1474568 | tf_op jit(solution)/shard_map/ppermute | solution.py:38
  100.6 7.2 %near_product.3.refs_4_ = bf16[864,1024]{1,0:T(8,128)(2,1)S(1)} custom-call(bf16[1024,3072]{1,0:T(8,128)(2,1)S(1)} %bitcast.13, bf16[144,3072]{1,0:T(8,128)(2,1)S(1)} %pad_maximum_fusion.1.refs_0_, bf16[144,3072]{1,0:T(8,128)(2,1)S(1)} %collective-permute-done.18.refs_1_, bf16[144,3072]{1,0:T(8,128)(2,1)S(1)} %collective-permute-done.11.refs_2_, ...), custom_call_target="tpu_custom_call" | custom-call | flops 1024 | bytes 1024 | tf_op jit(solution)/shard_map/near_product/pallas_call | solution.py:185
  107.8 8.4 %place.3 = bf16[2,1152,1024]{2,1,0:T(8,128)(2,1)} custom-call(s32[2,2,2048]{2,1,0:T(2,128)S(1)} %bitcast.26, s32[8,1152]{1,0:T(8,128)S(1)} %copy-done.10, bf16[1024,3072]{1,0:T(8,128)(2,1)S(1)} %bitcast.14, bf16[80,3072]{1,0:T(8,128)(2,1)S(1)} %collective-permute-done.16.refs_0_, ...), custom_call_target="tpu_custom_call", output_to_operand_aliasing={{}: (8, {})} | custom-call | flops 1024 | bytes 1024 | tf_op jit(solution)/shard_map/place/pallas_call | solution.py:253
  (66 shorter events, 14.3 us)
Async XLA Ops:
  7.9 17.5 %collective-permute-start.3 = (bf16[64,3072]{1,0:T(8,128)(2,1)S(1)}, bf16[64,3072]{1,0:T(8,128)(2,1)S(1)}, u32[]{:S(2)}, u32[]{:S(2)}) collective-permute-start(bf16[64,3072]{1,0:T(8,128)(2,1)S(1)} %get-tuple-element.57), channel_id=1, source_target_pairs={{32,0},{64,32},{96,64},{128,96},{160,128},{192,160},{224,192},{33,... | collective-permute-start | bytes 1179656 | tf_op jit(solution)/shard_map/ppermute | solution.py:43
  10.6 6.6 %collective-permute-start = (bf16[36,3072]{1,0:T(8,128)(2,1)S(1)}, bf16[36,3072]{1,0:T(8,128)(2,1)S(1)}, u32[]{:S(2)}, u32[]{:S(2)}) collective-permute-start(bf16[36,3072]{1,0:T(8,128)(2,1)S(1)} %get-tuple-element.53), channel_id=1, source_target_pairs={{0,8},{1,9},{2,10},{3,11},{4,12},{5,13},{6,14},{7,15},{8,16},{9,17... | collective-permute-start | bytes 663560 | tf_op jit(solution)/shard_map/ppermute | solution.py:38
  10.6 8.0 %collective-permute-start.1 = (bf16[36,3072]{1,0:T(8,128)(2,1)S(1)}, bf16[36,3072]{1,0:T(8,128)(2,1)S(1)}, u32[]{:S(2)}, u32[]{:S(2)}) collective-permute-start(bf16[36,3072]{1,0:T(8,128)(2,1)S(1)} %get-tuple-element.54), channel_id=1, source_target_pairs={{0,16},{1,17},{2,18},{3,19},{4,20},{5,21},{6,22},{7,23},{8,24},{9,... | collective-permute-start | bytes 663560 | tf_op jit(solution)/shard_map/ppermute | solution.py:38
  12.9 12.5 %collective-permute-start.2 = (bf16[36,3072]{1,0:T(8,128)(2,1)S(1)}, bf16[36,3072]{1,0:T(8,128)(2,1)S(1)}, u32[]{:S(2)}, u32[]{:S(2)}) collective-permute-start(bf16[36,3072]{1,0:T(8,128)(2,1)S(1)} %get-tuple-element.55), channel_id=1, source_target_pairs={{0,24},{1,25},{2,26},{3,27},{4,28},{5,29},{6,30},{7,31},{8,0},{9,1... | collective-permute-start | bytes 663560 | tf_op jit(solution)/shard_map/ppermute | solution.py:38
  25.5 22.0 %collective-permute-start.7 = (bf16[144,3072]{1,0:T(8,128)(2,1)S(1)}, bf16[144,3072]{1,0:T(8,128)(2,1)S(1)}, u32[]{:S(2)}, u32[]{:S(2)}) collective-permute-start(bf16[144,3072]{1,0:T(8,128)(2,1)S(1)} %pad_maximum_fusion.refs_0_), channel_id=1, source_target_pairs={{0,2},{1,3},{2,4},{3,5},{4,6},{5,7},{6,0},{7,1},{8,10},{9,11},{10,... | collective-permute-start | bytes 2654216 | tf_op jit(solution)/shard_map/ppermute | solution.py:38
  26.8 20.7 %collective-permute-start.8 = (bf16[144,3072]{1,0:T(8,128)(2,1)S(1)}, bf16[144,3072]{1,0:T(8,128)(2,1)S(1)}, u32[]{:S(2)}, u32[]{:S(2)}) collective-permute-start(bf16[144,3072]{1,0:T(8,128)(2,1)S(1)} %pad_maximum_fusion.refs_0_), channel_id=1, source_target_pairs={{0,6},{1,7},{2,0},{3,1},{4,2},{5,3},{6,4},{7,5},{8,14},{9,15},{10,... | collective-permute-start | bytes 2654216 | tf_op jit(solution)/shard_map/ppermute | solution.py:38
  29.0 6.4 %collective-permute-start.4 = (bf16[36,3072]{1,0:T(8,128)(2,1)S(1)}, bf16[36,3072]{1,0:T(8,128)(2,1)S(1)}, u32[]{:S(2)}, u32[]{:S(2)}) collective-permute-start(bf16[36,3072]{1,0:T(8,128)(2,1)S(1)} %get-tuple-element.60), channel_id=1, source_target_pairs={{0,8},{1,9},{2,10},{3,11},{4,12},{5,13},{6,14},{7,15},{8,16},{9,17... | collective-permute-start | bytes 663560 | tf_op jit(solution)/shard_map/ppermute | solution.py:38
  29.1 7.0 %collective-permute-start.5 = (bf16[36,3072]{1,0:T(8,128)(2,1)S(1)}, bf16[36,3072]{1,0:T(8,128)(2,1)S(1)}, u32[]{:S(2)}, u32[]{:S(2)}) collective-permute-start(bf16[36,3072]{1,0:T(8,128)(2,1)S(1)} %get-tuple-element.61), channel_id=1, source_target_pairs={{0,16},{1,17},{2,18},{3,19},{4,20},{5,21},{6,22},{7,23},{8,24},{9,... | collective-permute-start | bytes 663560 | tf_op jit(solution)/shard_map/ppermute | solution.py:38
  29.9 13.2 %collective-permute-start.6 = (bf16[36,3072]{1,0:T(8,128)(2,1)S(1)}, bf16[36,3072]{1,0:T(8,128)(2,1)S(1)}, u32[]{:S(2)}, u32[]{:S(2)}) collective-permute-start(bf16[36,3072]{1,0:T(8,128)(2,1)S(1)} %get-tuple-element.62), channel_id=1, source_target_pairs={{0,24},{1,25},{2,26},{3,27},{4,28},{5,29},{6,30},{7,31},{8,0},{9,1... | collective-permute-start | bytes 663560 | tf_op jit(solution)/shard_map/ppermute | solution.py:38
  47.5 4.9 %collective-permute-start.13 = (bf16[144,3072]{1,0:T(8,128)(2,1)S(1)}, bf16[144,3072]{1,0:T(8,128)(2,1)S(1)}, u32[]{:S(2)}, u32[]{:S(2)}) collective-permute-start(bf16[144,3072]{1,0:T(8,128)(2,1)S(1)} %pad_maximum_fusion.refs_0_), channel_id=1, source_target_pairs={{0,1},{1,0},{2,3},{3,2},{4,5},{5,4},{6,7},{7,6},{8,9},{9,8},{10,11... | collective-permute-start | bytes 2654216 | tf_op jit(solution)/shard_map/ppermute | solution.py:38
  48.9 3.7 %collective-permute-start.14 = (bf16[144,3072]{1,0:T(8,128)(2,1)S(1)}, bf16[144,3072]{1,0:T(8,128)(2,1)S(1)}, u32[]{:S(2)}, u32[]{:S(2)}) collective-permute-start(bf16[144,3072]{1,0:T(8,128)(2,1)S(1)} %collective-permute-done.7.refs_2_), channel_id=1, source_target_pairs={{0,1},{1,0},{2,3},{3,2},{4,5},{5,4},{6,7},{7,6},{8,9},{9,8},{10,11... | collective-permute-start | bytes 2654216 | tf_op jit(solution)/shard_map/ppermute | solution.py:38
  48.9 8.0 %collective-permute-start.15 = (bf16[144,3072]{1,0:T(8,128)(2,1)S(1)}, bf16[144,3072]{1,0:T(8,128)(2,1)S(1)}, u32[]{:S(2)}, u32[]{:S(2)}) collective-permute-start(bf16[144,3072]{1,0:T(8,128)(2,1)S(1)} %collective-permute-done.8.refs_4_), channel_id=1, source_target_pairs={{0,1},{1,0},{2,3},{3,2},{4,5},{5,4},{6,7},{7,6},{8,9},{9,8},{10,11... | collective-permute-start | bytes 2654216 | tf_op jit(solution)/shard_map/ppermute | solution.py:38
  49.6 33.1 %collective-permute-start.11 = (bf16[144,3072]{1,0:T(8,128)(2,1)S(1)}, bf16[144,3072]{1,0:T(8,128)(2,1)S(1)}, u32[]{:S(2)}, u32[]{:S(2)}) collective-permute-start(bf16[144,3072]{1,0:T(8,128)(2,1)S(1)} %pad_maximum_fusion.1.refs_0_), channel_id=1, source_target_pairs={{0,2},{1,3},{2,4},{3,5},{4,6},{5,7},{6,0},{7,1},{8,10},{9,11},{10,... | collective-permute-start | bytes 2654216 | tf_op jit(solution)/shard_map/ppermute | solution.py:38
  50.9 31.8 %collective-permute-start.12 = (bf16[144,3072]{1,0:T(8,128)(2,1)S(1)}, bf16[144,3072]{1,0:T(8,128)(2,1)S(1)}, u32[]{:S(2)}, u32[]{:S(2)}) collective-permute-start(bf16[144,3072]{1,0:T(8,128)(2,1)S(1)} %pad_maximum_fusion.1.refs_0_), channel_id=1, source_target_pairs={{0,6},{1,7},{2,0},{3,1},{4,2},{5,3},{6,4},{7,5},{8,14},{9,15},{10,... | collective-permute-start | bytes 2654216 | tf_op jit(solution)/shard_map/ppermute | solution.py:38
  52.5 30.2 %collective-permute-start.9 = (bf16[80,3072]{1,0:T(8,128)(2,1)S(1)}, bf16[80,3072]{1,0:T(8,128)(2,1)S(1)}, u32[]{:S(2)}, u32[]{:S(2)}) collective-permute-start(bf16[80,3072]{1,0:T(8,128)(2,1)S(1)} %slice.12), channel_id=1, source_target_pairs={{0,2},{1,3},{2,4},{3,5},{4,6},{5,7},{6,0},{7,1},{8,10},{9,11},{10,... | collective-permute-start | bytes 1474568 | tf_op jit(solution)/shard_map/ppermute | solution.py:38
  52.6 27.6 %collective-permute-start.10 = (bf16[64,3072]{1,0:T(8,128)(2,1)S(1)}, bf16[64,3072]{1,0:T(8,128)(2,1)S(1)}, u32[]{:S(2)}, u32[]{:S(2)}) collective-permute-start(bf16[64,3072]{1,0:T(8,128)(2,1)S(1)} %slice.13), channel_id=1, source_target_pairs={{0,6},{1,7},{2,0},{3,1},{4,2},{5,3},{6,4},{7,5},{8,14},{9,15},{10,... | collective-permute-start | bytes 1179656 | tf_op jit(solution)/shard_map/ppermute | solution.py:38
  82.7 2.9 %collective-permute-start.21 = (bf16[80,3072]{1,0:T(8,128)(2,1)S(1)}, bf16[80,3072]{1,0:T(8,128)(2,1)S(1)}, u32[]{:S(2)}, u32[]{:S(2)}) collective-permute-start(bf16[80,3072]{1,0:T(8,128)(2,1)S(1)} %collective-permute-done.9.refs_0_), channel_id=1, source_target_pairs={{0,1},{1,0},{2,3},{3,2},{4,5},{5,4},{6,7},{7,6},{8,9},{9,8},{10,11... | collective-permute-start | bytes 1474568 | tf_op jit(solution)/shard_map/ppermute | solution.py:38
  83.6 15.6 %collective-permute-start.18 = (bf16[144,3072]{1,0:T(8,128)(2,1)S(1)}, bf16[144,3072]{1,0:T(8,128)(2,1)S(1)}, u32[]{:S(2)}, u32[]{:S(2)}) collective-permute-start(bf16[144,3072]{1,0:T(8,128)(2,1)S(1)} %pad_maximum_fusion.1.refs_0_), channel_id=1, source_target_pairs={{0,1},{1,0},{2,3},{3,2},{4,5},{5,4},{6,7},{7,6},{8,9},{9,8},{10,11... | collective-permute-start | bytes 2654216 | tf_op jit(solution)/shard_map/ppermute | solution.py:38
  84.0 15.2 %collective-permute-start.19 = (bf16[144,3072]{1,0:T(8,128)(2,1)S(1)}, bf16[144,3072]{1,0:T(8,128)(2,1)S(1)}, u32[]{:S(2)}, u32[]{:S(2)}) collective-permute-start(bf16[144,3072]{1,0:T(8,128)(2,1)S(1)} %collective-permute-done.11.refs_2_), channel_id=1, source_target_pairs={{0,1},{1,0},{2,3},{3,2},{4,5},{5,4},{6,7},{7,6},{8,9},{9,8},{10,11... | collective-permute-start | bytes 2654216 | tf_op jit(solution)/shard_map/ppermute | solution.py:38
  84.1 15.1 %collective-permute-start.20 = (bf16[144,3072]{1,0:T(8,128)(2,1)S(1)}, bf16[144,3072]{1,0:T(8,128)(2,1)S(1)}, u32[]{:S(2)}, u32[]{:S(2)}) collective-permute-start(bf16[144,3072]{1,0:T(8,128)(2,1)S(1)} %collective-permute-done.12.refs_4_), channel_id=1, source_target_pairs={{0,1},{1,0},{2,3},{3,2},{4,5},{5,4},{6,7},{7,6},{8,9},{9,8},{10,11... | collective-permute-start | bytes 2654216 | tf_op jit(solution)/shard_map/ppermute | solution.py:38
  85.5 13.6 %collective-permute-start.16 = (bf16[80,3072]{1,0:T(8,128)(2,1)S(1)}, bf16[80,3072]{1,0:T(8,128)(2,1)S(1)}, u32[]{:S(2)}, u32[]{:S(2)}) collective-permute-start(bf16[80,3072]{1,0:T(8,128)(2,1)S(1)} %slice.14), channel_id=1, source_target_pairs={{0,2},{1,3},{2,4},{3,5},{4,6},{5,7},{6,0},{7,1},{8,10},{9,11},{10,... | collective-permute-start | bytes 1474568 | tf_op jit(solution)/shard_map/ppermute | solution.py:38
  85.6 11.4 %collective-permute-start.17 = (bf16[64,3072]{1,0:T(8,128)(2,1)S(1)}, bf16[64,3072]{1,0:T(8,128)(2,1)S(1)}, u32[]{:S(2)}, u32[]{:S(2)}) collective-permute-start(bf16[64,3072]{1,0:T(8,128)(2,1)S(1)} %slice.15), channel_id=1, source_target_pairs={{0,6},{1,7},{2,0},{3,1},{4,2},{5,3},{6,4},{7,5},{8,14},{9,15},{10,... | collective-permute-start | bytes 1179656 | tf_op jit(solution)/shard_map/ppermute | solution.py:38
  99.2 8.6 %collective-permute-start.23 = (bf16[80,3072]{1,0:T(8,128)(2,1)S(1)}, bf16[80,3072]{1,0:T(8,128)(2,1)S(1)}, u32[]{:S(2)}, u32[]{:S(2)}) collective-permute-start(bf16[80,3072]{1,0:T(8,128)(2,1)S(1)} %collective-permute-done.16.refs_0_), channel_id=1, source_target_pairs={{0,1},{1,0},{2,3},{3,2},{4,5},{5,4},{6,7},{7,6},{8,9},{9,8},{10,11... | collective-permute-start | bytes 1474568 | tf_op jit(solution)/shard_map/ppermute | solution.py:38
  100.5 7.3 %collective-permute-start.24 = (bf16[64,3072]{1,0:T(8,128)(2,1)S(1)}, bf16[64,3072]{1,0:T(8,128)(2,1)S(1)}, u32[]{:S(2)}, u32[]{:S(2)}) collective-permute-start(bf16[64,3072]{1,0:T(8,128)(2,1)S(1)} %collective-permute-done.17.refs_1_), channel_id=1, source_target_pairs={{0,1},{1,0},{2,3},{3,2},{4,5},{5,4},{6,7},{7,6},{8,9},{9,8},{10,11... | collective-permute-start | bytes 1179656 | tf_op jit(solution)/shard_map/ppermute | solution.py:38
  (14 other events, 196.4 us)

commit v2 on v1

v2 whole, which is shorter than its diff:
```python
import functools

import jax
import jax.numpy as jnp
import numpy as np
from jax import lax
from jax.experimental import pallas as pl
from jax.experimental.pallas import tpu as pltpu
from jax.sharding import PartitionSpec as P

TICKS = 2
CAP = 36
XS, YS, CORES = 4, 4, 2
EP = XS * YS * CORES
TOKENS = 64
D = 3072
HID = 1024
MAXP = EP * CAP
BLOCK = YS * CAP
HEAD = 80
DYS = (0, 1, 3, 2)
GROUP = CORES * BLOCK
STEP = 128
PLACED = 384
ORDER = ((0, 0), (1, 0), (3, 0), (0, 1), (1, 1), (3, 1), (2, 0), (2, 1))
VMEM = pl.BlockSpec(memory_space=pltpu.VMEM)
ANY = pl.BlockSpec(memory_space=pl.ANY)
HBM = pl.BlockSpec(memory_space=pltpu.HBM)
CHEAP = pl.CostEstimate(flops=1024, bytes_accessed=1024, transcendentals=0)
SOME = pl.CostEstimate(flops=1200 << 20, bytes_accessed=1024, transcendentals=0)
NT = (((1,), (1,)), ((), ()))


def hop(shard, dy=0, dx=0, dc=0):
    pairs = []
    for y in range(YS):
        for x in range(XS):
            for c in range(CORES):
                to = (((y + dy) % YS) * XS + (x + dx) % XS) * CORES + (c + dc) % CORES
                pairs.append(((y * XS + x) * CORES + c, to))
    return lax.ppermute(shard, "ep", pairs)


def down(shard):
    n = lax.axis_size("section")
    return lax.ppermute(shard, "section", [(i, i - 1) for i in range(1, n)])


def front_kernel(moment, count, ids_hbm, share_hbm, router_hbm, gap_hbm, *refs):
    grads, outs = refs[:count], refs[-14:-8]
    ids_ref, share_ref, router_ref, gap_ref, grads_ref, parts_ref, departing_ref, sems = refs[-8:]
    pairs = [(ids_hbm.at[moment], ids_ref), (share_hbm, share_ref)]
    pairs += [(grads[i], grads_ref.at[i]) for i in range(count)]
    pairs += [(gap_hbm.at[moment], gap_ref), (router_hbm, router_ref)]
    loads = [pltpu.make_async_copy(source, to, sems.at[i]) for i, (source, to) in enumerate(pairs)]
    for load in loads:
        load.start()
    for load in loads[: 2 + count]:
        load.wait()
    me = lax.axis_index("ep")
    both = ids_ref[:, pl.ds(pl.multiple_of((me // 2) * 128, 128), 128)].astype(jnp.float32)
    own = jnp.where(me % 2 == 0, both[:, :TOKENS], both[:, TOKENS:])
    first, second = own[0:1], own[1:2]
    share = share_ref[moment : moment + 1, :]
    gradient = grads_ref[0]
    if count == 2:
        last = lax.axis_index("section") == lax.axis_size("section") - 1
        gradient = jnp.where(last, gradient, grads_ref[1])

    my_y = (me // (XS * CORES)).astype(jnp.float32)
    experts = lax.broadcasted_iota(jnp.int32, (8, TOKENS), 0).astype(jnp.float32)
    is_first, is_second = experts == first, experts == second
    chosen = (is_first | is_second).astype(jnp.float32).astype(jnp.bfloat16)
    rows = lax.broadcasted_iota(jnp.int32, (TOKENS, TOKENS), 0)
    columns = lax.broadcasted_iota(jnp.int32, (TOKENS, TOKENS), 1)
    before = (rows < columns).astype(jnp.float32).astype(jnp.bfloat16)
    ranks = jnp.dot(chosen, before, preferred_element_type=jnp.float32)

    def placed(expert, mask):
        relative = expert - my_y
        relative = jnp.where(relative < 0, relative + YS, relative)
        return relative * CAP + jnp.sum(jnp.where(mask, ranks, 0.0), 0, keepdims=True)

    place_1, place_2 = placed(first, is_first), placed(second, is_second)
    slots = lax.broadcasted_iota(jnp.int32, (CAP, TOKENS), 0).astype(jnp.float32)
    stores = []
    for j in range(YS):
        one, two = slots + j * CAP == place_1, slots + j * CAP == place_2
        weight = jnp.sum(jnp.where(one, share, 0.0) + jnp.where(two, 1.0 - share, 0.0), 1, keepdims=True)
        placing = (one | two).astype(jnp.float32).astype(jnp.bfloat16)
        gathered = jnp.dot(placing, gradient, preferred_element_type=jnp.float32)
        parts_ref[j] = (gathered * weight).astype(jnp.bfloat16)
        stores.append(pltpu.make_async_copy(parts_ref.at[j], outs[j], sems.at[4 + count + j]))
        stores[j].start()

    def upright(row):
        return jnp.sum(jnp.where(rows == columns, row, 0.0), 1, keepdims=True)

    for load in loads[2 + count :]:
        load.wait()
    first, second, share = upright(first), upright(second), upright(share)
    gradient = gradient.astype(jnp.float32)
    gap_dot = jnp.sum(gradient * gap_ref[...].astype(jnp.float32), 1, keepdims=True)
    logit_grad = share * (1.0 - share) * gap_dot
    term = jnp.zeros((TOKENS, D), jnp.float32)
    for e in range(YS):
        sign = jnp.where(first == e, 1.0, 0.0) - jnp.where(second == e, 1.0, 0.0)
        term = term + (logit_grad * sign) * router_ref[e : e + 1, :]
    departing_ref[...] = (gradient + term).astype(jnp.bfloat16)
    for to in (outs[YS].at[moment], outs[YS + 1]):
        stores.append(pltpu.make_async_copy(departing_ref, to, sems.at[4 + count + len(stores)]))
        stores[-1].start()
    for store in stores:
        store.wait()


def front(moment, ids, share, router_rows, gap, grads, departs):
    more = [] if departs is None else [departs]
    count = len(grads)
    return pl.pallas_call(
        functools.partial(front_kernel, moment, count),
        out_shape=[jax.ShapeDtypeStruct((CAP, D), jnp.bfloat16)] * YS
        + [
            jax.ShapeDtypeStruct((TICKS, TOKENS, D), jnp.bfloat16),
            jax.ShapeDtypeStruct((TOKENS, D), jnp.bfloat16),
        ],
        in_specs=[HBM] * (4 + count + len(more)),
        out_specs=[HBM] * (YS + 2),
        scratch_shapes=[
            pltpu.VMEM((2, EP * TOKENS), jnp.int32),
            pltpu.VMEM((TICKS, TOKENS), jnp.float32),
            pltpu.VMEM((YS, D), jnp.float32),
            pltpu.VMEM((TOKENS, D), jnp.bfloat16),
            pltpu.VMEM((count, TOKENS, D), jnp.bfloat16),
            pltpu.VMEM((YS, CAP, D), jnp.bfloat16),
            pltpu.VMEM((TOKENS, D), jnp.bfloat16),
            pltpu.SemaphoreType.DMA((4 + count + YS + 2,)),
        ],
        input_output_aliases={4 + count: YS} if more else {},
        compiler_params=pltpu.CompilerParams(vmem_limit_bytes=(16 if more else 60) << 20),
        cost_estimate=CHEAP,
        name="front",
    )(ids, share, router_rows, gap, *grads, *more)


def load_rows(pieces, rows_ref, sems):
    copies, begin = [], 0
    for i, piece in enumerate(pieces):
        size = piece.shape[0]
        copies.append((begin, pltpu.make_async_copy(piece, rows_ref.at[pl.ds(begin, size)], sems.at[i])))
        copies[i][1].start()
        begin += size
    return copies


def multiply(copies, rows_ref, down_ref, product_ref, base):
    for begin in range(0, rows_ref.shape[0], GROUP):
        for at, copy in copies:
            if begin <= at < begin + GROUP:
                copy.wait()
        product = lax.dot_general(
            rows_ref[pl.ds(begin, GROUP), :], down_ref[...], NT, preferred_element_type=jnp.float32
        )
        product_ref[pl.ds(base + begin, GROUP), :] = product.astype(jnp.bfloat16)


def near_kernel(count, down_ref, *refs):
    product_ref, rows_ref, sems = refs[count:]
    multiply(load_rows(refs[:count], rows_ref, sems), rows_ref, down_ref, product_ref, 0)


def near_product(pieces, down_rows):
    total = sum(p.shape[0] for p in pieces)
    return pl.pallas_call(
        functools.partial(near_kernel, len(pieces)),
        out_shape=jax.ShapeDtypeStruct((total, HID), jnp.bfloat16),
        in_specs=[VMEM] + [ANY] * len(pieces),
        out_specs=VMEM,
        scratch_shapes=[pltpu.VMEM((total, D), jnp.bfloat16), pltpu.SemaphoreType.DMA((len(pieces),))],
        compiler_params=pltpu.CompilerParams(vmem_limit_bytes=24 << 20),
        cost_estimate=CHEAP,
        name="near_product",
    )(down_rows, *pieces)


def plan_kernel(ids_ref, table_ref, *outs):
    me = lax.axis_index("ep")
    my_y, my_x, my_c = me // (XS * CORES), (me // CORES) % XS, me % CORES
    table = table_ref[...]
    source = (
        ((my_y - table[0:1]) & (YS - 1)) * (XS * CORES)
        + ((my_x - table[1:2]) & (XS - 1)) * CORES
        + ((my_c - table[2:3]) & (CORES - 1))
    )
    slot = table[3:4].astype(jnp.float32)
    device = lax.broadcasted_iota(jnp.int32, (EP, MAXP), 0)
    ahead = (device < source).astype(jnp.float32).astype(jnp.bfloat16)
    itself = (device == source).astype(jnp.float32).astype(jnp.bfloat16)
    owner = lax.broadcasted_iota(jnp.int32, (EP, EP * TOKENS), 1) // TOKENS
    owned = (owner == lax.broadcasted_iota(jnp.int32, (EP, EP * TOKENS), 0)).astype(jnp.float32).astype(jnp.bfloat16)
    for moment in range(TICKS):
        named = (ids_ref[moment] == my_y).astype(jnp.float32)
        named = jnp.broadcast_to(named[0:1] + named[1:2], (8, EP * TOKENS)).astype(jnp.bfloat16)
        counts = lax.dot_general(named, owned, NT, preferred_element_type=jnp.float32).astype(jnp.bfloat16)
        offset = jnp.dot(counts, ahead, preferred_element_type=jnp.float32)[0:1]
        amount = jnp.dot(counts, itself, preferred_element_type=jnp.float32)[0:1]
        target = jnp.where(slot < amount, offset + slot, -1.0).astype(jnp.int32)

        @pl.loop(0, MAXP // STEP)
        def _(k):
            at = pl.multiple_of(k * STEP, STEP)
            here = lax.broadcasted_iota(jnp.int32, (STEP, MAXP), 0) + at
            outs[moment][pl.ds(at, STEP), :] = (here == target).astype(jnp.float32).astype(jnp.bfloat16)


def plan(ids):
    columns = [(dy, dx, dc, slot) for dx, dc in ORDER for dy in DYS for slot in range(CAP)]
    table = np.zeros((8, MAXP), np.int32)
    table[:4] = np.array(columns, np.int32).T
    return pl.pallas_call(
        plan_kernel,
        out_shape=[jax.ShapeDtypeStruct((MAXP, MAXP), jnp.bfloat16)] * TICKS,
        in_specs=[VMEM] * 2,
        out_specs=[VMEM] * TICKS,
        compiler_params=pltpu.CompilerParams(vmem_limit_bytes=16 << 20),
        cost_estimate=CHEAP,
        name="plan",
    )(ids, jnp.asarray(table))


def place_kernel(moment, count, placing_ref, down_ref, *refs):
    pieces, near_ref = refs[:count], refs[count]
    out_ref, rows_ref, product_ref, placed_ref, sems = refs[-5:]
    copies = load_rows(pieces, rows_ref, sems)
    base = MAXP - rows_ref.shape[0]
    back = pltpu.make_async_copy(near_ref, product_ref.at[pl.ds(0, base)], sems.at[count])
    back.start()
    multiply(copies, rows_ref, down_ref, product_ref, base)
    back.wait()
    stores = []
    for k in range(MAXP // PLACED):
        part = pl.ds(k * PLACED, PLACED)
        placed = jnp.dot(placing_ref[part, :], product_ref[...], preferred_element_type=jnp.float32)
        placed_ref[part, :] = placed.astype(jnp.bfloat16)
        stores.append(
            pltpu.make_async_copy(placed_ref.at[part], out_ref.at[moment, part], sems.at[count + 1 + k])
        )
        stores[k].start()
    for store in stores:
        store.wait()


def place(moment, placing, pieces, near, down_rows, hidden):
    more = [] if hidden is None else [hidden]
    return pl.pallas_call(
        functools.partial(place_kernel, moment, len(pieces)),
        out_shape=jax.ShapeDtypeStruct((TICKS, MAXP, HID), jnp.bfloat16),
        in_specs=[VMEM] * 2 + [ANY] * (len(pieces) + 1 + len(more)),
        out_specs=ANY,
        scratch_shapes=[
            pltpu.VMEM((sum(p.shape[0] for p in pieces), D), jnp.bfloat16),
            pltpu.VMEM((MAXP, HID), jnp.bfloat16),
            pltpu.VMEM((MAXP, HID), jnp.bfloat16),
            pltpu.SemaphoreType.DMA((len(pieces) + 1 + MAXP // PLACED,)),
        ],
        input_output_aliases={3 + len(pieces): 0} if more else {},
        compiler_params=pltpu.CompilerParams(vmem_limit_bytes=24 << 20),
        cost_estimate=SOME,
        name="place",
    )(placing, down_rows, *pieces, near, *more)


def spread(parts):
    return {j: hop(parts[j], dy=j) for j in (1, 3, 2)}


def joined(own, came):
    return jnp.concatenate([own, came[1], came[3], came[2]], 0)


def beside(block):
    return {dx: hop(block, dx=dx) for dx in (1, 3)}


def opposite(near):
    return hop(near[1][:HEAD], dx=1), hop(near[3][HEAD:], dx=3)


def swapped(tree):
    return jax.tree.map(lambda p: hop(p, dc=1), tree)


def local(arriving, top_grad, expert_ids, first_share, out_gap, router_weight, down_weight):
    tie = lax.optimization_barrier
    ids = jnp.swapaxes(expert_ids[0], 1, 2)
    share, gap, router_rows, down_rows = first_share[0], out_gap[0], router_weight[0], down_weight[0]

    *parts0, departs, departing = front(0, ids, share, router_rows, gap, [arriving[0]], None)
    placing = plan(ids)
    own0, came0, moved, placing = tie((parts0[0], spread(parts0), down(departing), placing))

    block0 = joined(own0, came0)
    near0 = beside(block0)
    *parts1, departs, _ = front(1, ids, share, router_rows, gap, [top_grad[0], moved], departs)
    own1, came1, block0, near0 = tie((parts1[0], spread(parts1), block0, near0))

    block1 = joined(own1, came1)
    far0 = opposite(near0)
    near1 = beside(block1)
    pieces = [block0, near0[1], near0[3]]
    product0 = near_product([*pieces, swapped(jnp.concatenate(pieces))], down_rows)
    hidden = place(0, placing[0], [*far0, *swapped(far0)], product0, down_rows, None)
    block1, near1, hidden = tie((block1, near1, hidden))

    far1 = opposite(near1)
    pieces = [block1, near1[1], near1[3]]
    product1 = near_product([*pieces, swapped(jnp.concatenate(pieces))], down_rows)
    far1, product1 = tie((far1, product1))

    hidden = place(1, placing[1], [*far1, *swapped(far1)], product1, down_rows, hidden)
    return departs[None], hidden[None]


def solution(mesh):
    placed = (
        P("section", "ep", None),
        P(None, "ep", None),
        P("section", None, None, None),
        P("section", None, "ep"),
        P("section", None, "ep", None),
        P("section", None, None),
        P("section", "ep", None),
    )
    return jax.shard_map(
        local,
        mesh=mesh,
        in_specs=placed,
        out_specs=(P("section", None, "ep", None), P("section", None, "ep", None)),
        check_vma=False,
    )
```

time: 117 us -> 106 us (0.906)
  waiting for transfers between devices: 51.1 us -> 42.1 us
  local copies, waits for them, and re-layouts: 5.5 us -> 1.68 us
  Pallas kernels: 35.2 us -> 37.7 us
  starting transfers between devices: 23.2 us -> 21.1 us
  other arithmetic: 0.32 us -> 1.61 us
    ppermute x24 -> x20, waiting for transfers between devices: 51.1 us -> 42.1 us  [hop(): return lax.ppermute(shard, 'ep', pairs)]
    pallas_call x4 -> x3, Pallas kernels: 3.94 us -> 9.21 us  [the longest x2 7.51 us: front(): pl.pallas_call(functools.partial(front_kernel, moment, count), out_shape=...]
    unnamed x26 -> x18, local copies, waits for them, and re-layouts: 5.38 us -> 1.56 us
    ppermute x24 -> x20, starting transfers between devices: 20.6 us -> 18.5 us  [hop(): return lax.ppermute(shard, 'ep', pairs)]
    pallas_call x2, Pallas kernels: 16.8 us -> 15.1 us  [place(): pl.pallas_call(functools.partial(place_kernel, moment, len(pieces)), out_...]
  transfers between devices with their start and end apart: 25 -> 21, of which waited for: 11 -> 14; matrix products, arithmetic and copies ran while one was open for 0% -> 0% of each run, Pallas kernels for 21% -> 26%
where the time goes in v2:
time: 106 us; the launch traced here: 105 us
  waiting for transfers between devices  42.1 us (40%)
  Pallas kernels  37.7 us (36%)
  starting transfers between devices  21.1 us (20%)
  local copies, waits for them, and re-layouts  1.68 us (2%)
  other arithmetic  1.61 us (2%)
  between operations  1.06 us (1%)
    ppermute x20, waiting for transfers between devices, hop(): return lax.ppermute(shard, 'ep', pairs)  42.1 us
    ppermute x20, starting transfers between devices, hop(): return lax.ppermute(shard, 'ep', pairs)  18.5 us
    pallas_call x2, Pallas kernels, place(): pl.pallas_call(functools.partial(place_kernel, moment, len(pieces)), out_...  15.1 us
    pallas_call x2, Pallas kernels, near_product(): pl.pallas_call(functools.partial(near_kernel, len(pieces)), out_shape=jax...  13.3 us
    pallas_call x2, Pallas kernels, front(): pl.pallas_call(functools.partial(front_kernel, moment, count), out_shape=...  7.51 us
    ppermute x1, starting transfers between devices, down(): return lax.ppermute(shard, 'section', [(i, i - 1) for i in range(1, n)])  2.65 us
  transfers between devices with their start and end apart: 21, of which 14 were waited for; matrix products, arithmetic and copies ran while one was open for 0% of the time, Pallas kernels for 26%

profile of v2, /device:TPU:249, one launch (start us, length us, event | category | flops | bytes accessed | tf_op | source)
XLA Modules:
  0.0 105.3 jit_solution(11804535637602535211)
XLA Ops:
  0.7 3.2 %front.2 = (bf16[36,3072]{1,0:T(8,128)(2,1)}, bf16[36,3072]{1,0:T(8,128)(2,1)}, bf16[36,3072]{1,0:T(8,128)(2,1)}, bf16[36,3072]{1,0:T(8,128)(2,1)}, bf16[2,64,30...) custom-call(s32[2,2,2048]{2,1,0:T(2,128)} %bitcast.20, f32[2,64]{1,0:T(2,128)} %bitcast.25, f32[4,3072]{1,0:T(4,128)} %bitcast.23, ...), custom_call_target="tpu_custom_call" | custom-call | flops 1024 | bytes 1024 | tf_op jit(solution)/shard_map/front/pallas_call | solution.py:120
  3.9 2.7 %collective-permute-start.3 = (bf16[64,3072]{1,0:T(8,128)(2,1)}, bf16[64,3072]{1,0:T(8,128)(2,1)S(1)}, u32[]{:S(2)}, u32[]{:S(2)}) collective-permute-start(bf16[64,3072]{1,0:T(8,128)(2,1)} %get-tuple-element.40), channel_id=1, source_target_pairs={{32,0},{64,32},{96,64},{128,96},{160,128},{192,160},{224,192},{33,... | collective-permute-start | bytes 1179656 | tf_op jit(solution)/shard_map/ppermute | solution.py:46
  6.6 2.2 %collective-permute-start.1 = (bf16[36,3072]{1,0:T(8,128)(2,1)}, bf16[36,3072]{1,0:T(8,128)(2,1)S(1)}, u32[]{:S(2)}, u32[]{:S(2)}) collective-permute-start(bf16[36,3072]{1,0:T(8,128)(2,1)} %get-tuple-element.38), channel_id=1, source_target_pairs={{0,16},{1,17},{2,18},{3,19},{4,20},{5,21},{6,22},{7,23},{8,24},{9,... | collective-permute-start | bytes 663560 | tf_op jit(solution)/shard_map/ppermute | solution.py:41
  10.4 1.7 %plan.1 = (bf16[1152,1152]{1,0:T(8,128)(2,1)S(1)}, bf16[1152,1152]{1,0:T(8,128)(2,1)S(1)}) custom-call(s32[2,2,2048]{2,1,0:T(2,128)S(1)} %bitcast.21, s32[8,1152]{1,0:T(8,128)S(1)} %copy-done.5), custom_call_target="tpu_custom_call" | custom-call | flops 1024 | bytes 1024 | tf_op jit(solution)/shard_map/plan/pallas_call | solution.py:220
  13.3 1.5 %collective-permute-done.1 = bf16[36,3072]{1,0:T(8,128)(2,1)S(1)} collective-permute-done((bf16[36,3072]{1,0:T(8,128)(2,1)}, bf16[36,3072]{1,0:T(8,128)(2,1)S(1)}, u32[]{:S(2)}, u32[]{:S(2)}) %collective-permute-start.1) | collective-permute-done | bytes 221216 | tf_op jit(solution)/shard_map/ppermute | solution.py:41
  14.8 6.7 %collective-permute-done.2 = bf16[36,3072]{1,0:T(8,128)(2,1)S(1)} collective-permute-done((bf16[36,3072]{1,0:T(8,128)(2,1)}, bf16[36,3072]{1,0:T(8,128)(2,1)S(1)}, u32[]{:S(2)}, u32[]{:S(2)}) %collective-permute-start.2) | collective-permute-done | bytes 221216 | tf_op jit(solution)/shard_map/ppermute | solution.py:41
  22.7 1.3 %collective-permute-start.7 = (bf16[144,3072]{1,0:T(8,128)(2,1)S(1)}, bf16[144,3072]{1,0:T(8,128)(2,1)S(1)}, u32[]{:S(2)}, u32[]{:S(2)}) collective-permute-start(bf16[144,3072]{1,0:T(8,128)(2,1)S(1)} %pad_maximum_fusion.2.refs_0_), channel_id=1, source_target_pairs={{0,2},{1,3},{2,4},{3,5},{4,6},{5,7},{6,0},{7,1},{8,10},{9,11},{10,... | collective-permute-start | bytes 2654216 | tf_op jit(solution)/shard_map/ppermute | solution.py:41
  23.9 1.5 %collective-permute-start.8 = (bf16[144,3072]{1,0:T(8,128)(2,1)S(1)}, bf16[144,3072]{1,0:T(8,128)(2,1)S(1)}, u32[]{:S(2)}, u32[]{:S(2)}) collective-permute-start(bf16[144,3072]{1,0:T(8,128)(2,1)S(1)} %pad_maximum_fusion.2.refs_0_), channel_id=1, source_target_pairs={{0,6},{1,7},{2,0},{3,1},{4,2},{5,3},{6,4},{7,5},{8,14},{9,15},{10,... | collective-permute-start | bytes 2654216 | tf_op jit(solution)/shard_map/ppermute | solution.py:41
  25.4 4.3 %front.3 = (bf16[36,3072]{1,0:T(8,128)(2,1)S(1)}, bf16[36,3072]{1,0:T(8,128)(2,1)S(1)}, bf16[36,3072]{1,0:T(8,128)(2,1)S(1)}, bf16[36,3072]{1,0:T(8,128)(2,1)S(1...) custom-call(s32[2,2,2048]{2,1,0:T(2,128)S(1)} %bitcast.22, ...), custom_call_target="tpu_custom_call", output_to_operand_aliasing={{4}: (6, {})} | custom-call | flops 1024 | bytes 1024 | tf_op jit(solution)/shard_map/front/pallas_call | solution.py:120
  31.5 4.8 %collective-permute-done.4 = bf16[36,3072]{1,0:T(8,128)(2,1)S(1)} collective-permute-done((bf16[36,3072]{1,0:T(8,128)(2,1)S(1)}, bf16[36,3072]{1,0:T(8,128)(2,1)S(1)}, u32[]{:S(2)}, u32[]{:S(2)}) %collective-permute-start.4) | collective-permute-done | bytes 221216 | tf_op jit(solution)/shard_map/ppermute | solution.py:41
  36.9 7.0 %collective-permute-done.6 = bf16[36,3072]{1,0:T(8,128)(2,1)S(1)} collective-permute-done((bf16[36,3072]{1,0:T(8,128)(2,1)S(1)}, bf16[36,3072]{1,0:T(8,128)(2,1)S(1)}, u32[]{:S(2)}, u32[]{:S(2)}) %collective-permute-start.6) | collective-permute-done | bytes 221216 | tf_op jit(solution)/shard_map/ppermute | solution.py:41
  44.8 1.4 %collective-permute-start.15 = (bf16[432,3072]{1,0:T(8,128)(2,1)S(1)}, bf16[432,3072]{1,0:T(8,128)(2,1)S(1)}, u32[]{:S(2)}, u32[]{:S(2)}) collective-permute-start(bf16[432,3072]{1,0:T(8,128)(2,1)S(1)} %pad_maximum_fusion), channel_id=1, source_target_pairs={{0,1},{1,0},{2,3},{3,2},{4,5},{5,4},{6,7},{7,6},{8,9},{9,8},{10,11... | collective-permute-start | bytes 7962632 | tf_op jit(solution)/shard_map/ppermute | solution.py:41
  47.6 1.6 %collective-permute-start.12 = (bf16[64,3072]{1,0:T(8,128)(2,1)S(1)}, bf16[64,3072]{1,0:T(8,128)(2,1)S(1)}, u32[]{:S(2)}, u32[]{:S(2)}) collective-permute-start(bf16[64,3072]{1,0:T(8,128)(2,1)S(1)} %slice.13), channel_id=1, source_target_pairs={{0,6},{1,7},{2,0},{3,1},{4,2},{5,3},{6,4},{7,5},{8,14},{9,15},{10,... | collective-permute-start | bytes 1179656 | tf_op jit(solution)/shard_map/ppermute | solution.py:41
  49.4 1.5 %collective-permute-start.10 = (bf16[144,3072]{1,0:T(8,128)(2,1)S(1)}, bf16[144,3072]{1,0:T(8,128)(2,1)S(1)}, u32[]{:S(2)}, u32[]{:S(2)}) collective-permute-start(bf16[144,3072]{1,0:T(8,128)(2,1)S(1)} %pad_maximum_fusion.3.refs_0_), channel_id=1, source_target_pairs={{0,6},{1,7},{2,0},{3,1},{4,2},{5,3},{6,4},{7,5},{8,14},{9,15},{10,... | collective-permute-start | bytes 2654216 | tf_op jit(solution)/shard_map/ppermute | solution.py:41
  50.9 9.6 %collective-permute-done.11.refs_0_ = bf16[80,3072]{1,0:T(8,128)(2,1)S(1)} collective-permute-done((bf16[80,3072]{1,0:T(8,128)(2,1)S(1)}, bf16[80,3072]{1,0:T(8,128)(2,1)S(1)}, u32[]{:S(2)}, u32[]{:S(2)}) %collective-permute-start.11) | collective-permute-done | bytes 491552 | tf_op jit(solution)/shard_map/ppermute | solution.py:41
  61.7 6.7 %near_product.2.refs_4_ = bf16[864,1024]{1,0:T(8,128)(2,1)S(1)} custom-call(bf16[1024,3072]{1,0:T(8,128)(2,1)S(1)} %bitcast.13, bf16[144,3072]{1,0:T(8,128)(2,1)S(1)} %pad_maximum_fusion.2.refs_0_, bf16[144,3072]{1,0:T(8,128)(2,1)S(1)} %collective-permute-done.7.refs_1_, bf16[144,3072]{1,0:T(8,128)(2,1)S(1)} %collective-permute-done.8.refs_2_, ...), custom_call_target="tpu_custom_call" | custom-call | flops 1024 | bytes 1024 | tf_op jit(solution)/shard_map/near_product/pallas_call | solution.py:174
  68.4 7.5 %place.2.refs_5_ = bf16[2,1152,1024]{2,1,0:T(8,128)(2,1)} custom-call(bf16[1152,1152]{1,0:T(8,128)(2,1)S(1)} %get-tuple-element.59.placing_ref, bf16[1024,3072]{1,0:T(8,128)(2,1)S(1)} %bitcast.14, bf16[80,3072]{1,0:T(8,128)(2,1)S(1)} %collective-permute-done.11.refs_0_, bf16[64,3072]{1,0:T(8,128)(2,1)S(1)} %collective-permute-done.12.refs_1_, ...), custom_call_target="tpu_custom_call" | custom-call | flops 1258291200 | bytes 1024 | tf_op jit(solution)/shard_map/place/pallas_call | solution.py:255
  77.0 2.4 %collective-permute-done.9.refs_1_ = bf16[144,3072]{1,0:T(8,128)(2,1)S(1)} collective-permute-done((bf16[144,3072]{1,0:T(8,128)(2,1)S(1)}, bf16[144,3072]{1,0:T(8,128)(2,1)S(1)}, u32[]{:S(2)}, u32[]{:S(2)}) %collective-permute-start.9) | collective-permute-done | bytes 884768 | tf_op jit(solution)/shard_map/ppermute | solution.py:41
  80.7 3.0 %collective-permute-start.17 = (bf16[64,3072]{1,0:T(8,128)(2,1)S(1)}, bf16[64,3072]{1,0:T(8,128)(2,1)S(1)}, u32[]{:S(2)}, u32[]{:S(2)}) collective-permute-start(bf16[64,3072]{1,0:T(8,128)(2,1)S(1)} %slice.15), channel_id=1, source_target_pairs={{0,6},{1,7},{2,0},{3,1},{4,2},{5,3},{6,4},{7,5},{8,14},{9,15},{10,... | collective-permute-start | bytes 1179656 | tf_op jit(solution)/shard_map/ppermute | solution.py:41
  83.6 1.5 %collective-permute-done.18.refs_3_ = bf16[432,3072]{1,0:T(8,128)(2,1)S(1)} collective-permute-done((bf16[432,3072]{1,0:T(8,128)(2,1)S(1)}, bf16[432,3072]{1,0:T(8,128)(2,1)S(1)}, u32[]{:S(2)}, u32[]{:S(2)}) %collective-permute-start.18) | collective-permute-done | bytes 2654240 | tf_op jit(solution)/shard_map/ppermute | solution.py:41
  85.1 6.7 %near_product.3.refs_4_ = bf16[864,1024]{1,0:T(8,128)(2,1)S(1)} custom-call(bf16[1024,3072]{1,0:T(8,128)(2,1)S(1)} %bitcast.15, bf16[144,3072]{1,0:T(8,128)(2,1)S(1)} %pad_maximum_fusion.3.refs_0_, bf16[144,3072]{1,0:T(8,128)(2,1)S(1)} %collective-permute-done.9.refs_1_, bf16[144,3072]{1,0:T(8,128)(2,1)S(1)} %collective-permute-done.10.refs_2_, ...), custom_call_target="tpu_custom_call" | custom-call | flops 1024 | bytes 1024 | tf_op jit(solution)/shard_map/near_product/pallas_call | solution.py:174
  91.8 2.8 %collective-permute-done.16.refs_0_ = bf16[80,3072]{1,0:T(8,128)(2,1)S(1)} collective-permute-done((bf16[80,3072]{1,0:T(8,128)(2,1)S(1)}, bf16[80,3072]{1,0:T(8,128)(2,1)S(1)}, u32[]{:S(2)}, u32[]{:S(2)}) %collective-permute-start.16) | collective-permute-done | bytes 491552 | tf_op jit(solution)/shard_map/ppermute | solution.py:41
  95.5 2.0 %collective-permute-done.20.refs_3_ = bf16[64,3072]{1,0:T(8,128)(2,1)S(1)} collective-permute-done((bf16[64,3072]{1,0:T(8,128)(2,1)S(1)}, bf16[64,3072]{1,0:T(8,128)(2,1)S(1)}, u32[]{:S(2)}, u32[]{:S(2)}) %collective-permute-start.20) | collective-permute-done | bytes 393248 | tf_op jit(solution)/shard_map/ppermute | solution.py:41
  97.5 7.6 %place.3 = bf16[2,1152,1024]{2,1,0:T(8,128)(2,1)} custom-call(bf16[1152,1152]{1,0:T(8,128)(2,1)S(1)} %get-tuple-element.46.placing_ref, bf16[1024,3072]{1,0:T(8,128)(2,1)S(1)} %bitcast.16, bf16[80,3072]{1,0:T(8,128)(2,1)S(1)} %collective-permute-done.16.refs_0_, ...), custom_call_target="tpu_custom_call", output_to_operand_aliasing={{}: (7, {})} | custom-call | flops 1258291200 | bytes 1024 | tf_op jit(solution)/shard_map/place/pallas_call | solution.py:255
  (52 shorter events, 13.1 us)
Async XLA Ops:
  0.6 24.8 %copy-start.3 = (s32[1,2,2048,2]{2,3,1,0:T(2,128)S(1)}, s32[1,2,2048,2]{2,3,1,0:T(2,128)}, u32[]{:S(2)}) copy-start(s32[1,2,2048,2]{2,3,1,0:T(2,128)} %param.10) | copy-start | bytes 98308
  0.6 24.8 %copy-start.6 = (f32[1,2,64]{2,1,0:T(2,128)S(1)}, f32[1,2,64]{2,1,0:T(2,128)}, u32[]{:S(2)}) copy-start(f32[1,2,64]{2,1,0:T(2,128)} %param.11) | copy-start | bytes 1540
  3.9 17.7 %collective-permute-start.3 = (bf16[64,3072]{1,0:T(8,128)(2,1)}, bf16[64,3072]{1,0:T(8,128)(2,1)S(1)}, u32[]{:S(2)}, u32[]{:S(2)}) collective-permute-start(bf16[64,3072]{1,0:T(8,128)(2,1)} %get-tuple-element.40), channel_id=1, source_target_pairs={{32,0},{64,32},{96,64},{128,96},{160,128},{192,160},{224,192},{33,... | collective-permute-start | bytes 1179656 | tf_op jit(solution)/shard_map/ppermute | solution.py:46
  6.5 6.8 %collective-permute-start = (bf16[36,3072]{1,0:T(8,128)(2,1)}, bf16[36,3072]{1,0:T(8,128)(2,1)S(1)}, u32[]{:S(2)}, u32[]{:S(2)}) collective-permute-start(bf16[36,3072]{1,0:T(8,128)(2,1)} %get-tuple-element.37), channel_id=1, source_target_pairs={{0,8},{1,9},{2,10},{3,11},{4,12},{5,13},{6,14},{7,15},{8,16},{9,17... | collective-permute-start | bytes 663560 | tf_op jit(solution)/shard_map/ppermute | solution.py:41
  6.6 8.2 %collective-permute-start.1 = (bf16[36,3072]{1,0:T(8,128)(2,1)}, bf16[36,3072]{1,0:T(8,128)(2,1)S(1)}, u32[]{:S(2)}, u32[]{:S(2)}) collective-permute-start(bf16[36,3072]{1,0:T(8,128)(2,1)} %get-tuple-element.38), channel_id=1, source_target_pairs={{0,16},{1,17},{2,18},{3,19},{4,20},{5,21},{6,22},{7,23},{8,24},{9,... | collective-permute-start | bytes 663560 | tf_op jit(solution)/shard_map/ppermute | solution.py:41
  8.8 12.7 %collective-permute-start.2 = (bf16[36,3072]{1,0:T(8,128)(2,1)}, bf16[36,3072]{1,0:T(8,128)(2,1)S(1)}, u32[]{:S(2)}, u32[]{:S(2)}) collective-permute-start(bf16[36,3072]{1,0:T(8,128)(2,1)} %get-tuple-element.39), channel_id=1, source_target_pairs={{0,24},{1,25},{2,26},{3,27},{4,28},{5,29},{6,30},{7,31},{8,0},{9,1... | collective-permute-start | bytes 663560 | tf_op jit(solution)/shard_map/ppermute | solution.py:41
  22.7 22.0 %collective-permute-start.7 = (bf16[144,3072]{1,0:T(8,128)(2,1)S(1)}, bf16[144,3072]{1,0:T(8,128)(2,1)S(1)}, u32[]{:S(2)}, u32[]{:S(2)}) collective-permute-start(bf16[144,3072]{1,0:T(8,128)(2,1)S(1)} %pad_maximum_fusion.2.refs_0_), channel_id=1, source_target_pairs={{0,2},{1,3},{2,4},{3,5},{4,6},{5,7},{6,0},{7,1},{8,10},{9,11},{10,... | collective-permute-start | bytes 2654216 | tf_op jit(solution)/shard_map/ppermute | solution.py:41
  23.9 20.7 %collective-permute-start.8 = (bf16[144,3072]{1,0:T(8,128)(2,1)S(1)}, bf16[144,3072]{1,0:T(8,128)(2,1)S(1)}, u32[]{:S(2)}, u32[]{:S(2)}) collective-permute-start(bf16[144,3072]{1,0:T(8,128)(2,1)S(1)} %pad_maximum_fusion.2.refs_0_), channel_id=1, source_target_pairs={{0,6},{1,7},{2,0},{3,1},{4,2},{5,3},{6,4},{7,5},{8,14},{9,15},{10,... | collective-permute-start | bytes 2654216 | tf_op jit(solution)/shard_map/ppermute | solution.py:41
  25.4 36.3 %slice-start = ((s8[6291456]{0:T(1024)(128)(4,1)}), s8[4194304]{0:T(1024)(128)(4,1)S(1)}, s32[]{:S(2)}) async-start(s8[6291456]{0:T(1024)(128)(4,1)} %bitcast.11), calls=%async_computation | async-start | bytes 8388608
  29.8 6.5 %collective-permute-start.4 = (bf16[36,3072]{1,0:T(8,128)(2,1)S(1)}, bf16[36,3072]{1,0:T(8,128)(2,1)S(1)}, u32[]{:S(2)}, u32[]{:S(2)}) collective-permute-start(bf16[36,3072]{1,0:T(8,128)(2,1)S(1)} %get-tuple-element.48), channel_id=1, source_target_pairs={{0,8},{1,9},{2,10},{3,11},{4,12},{5,13},{6,14},{7,15},{8,16},{9,17... | collective-permute-start | bytes 663560 | tf_op jit(solution)/shard_map/ppermute | solution.py:41
  29.9 7.1 %collective-permute-start.5 = (bf16[36,3072]{1,0:T(8,128)(2,1)S(1)}, bf16[36,3072]{1,0:T(8,128)(2,1)S(1)}, u32[]{:S(2)}, u32[]{:S(2)}) collective-permute-start(bf16[36,3072]{1,0:T(8,128)(2,1)S(1)} %get-tuple-element.49), channel_id=1, source_target_pairs={{0,16},{1,17},{2,18},{3,19},{4,20},{5,21},{6,22},{7,23},{8,24},{9,... | collective-permute-start | bytes 663560 | tf_op jit(solution)/shard_map/ppermute | solution.py:41
  30.8 13.1 %collective-permute-start.6 = (bf16[36,3072]{1,0:T(8,128)(2,1)S(1)}, bf16[36,3072]{1,0:T(8,128)(2,1)S(1)}, u32[]{:S(2)}, u32[]{:S(2)}) collective-permute-start(bf16[36,3072]{1,0:T(8,128)(2,1)S(1)} %get-tuple-element.50), channel_id=1, source_target_pairs={{0,24},{1,25},{2,26},{3,27},{4,28},{5,29},{6,30},{7,31},{8,0},{9,1... | collective-permute-start | bytes 663560 | tf_op jit(solution)/shard_map/ppermute | solution.py:41
  44.8 16.8 %collective-permute-start.15 = (bf16[432,3072]{1,0:T(8,128)(2,1)S(1)}, bf16[432,3072]{1,0:T(8,128)(2,1)S(1)}, u32[]{:S(2)}, u32[]{:S(2)}) collective-permute-start(bf16[432,3072]{1,0:T(8,128)(2,1)S(1)} %pad_maximum_fusion), channel_id=1, source_target_pairs={{0,1},{1,0},{2,3},{3,2},{4,5},{5,4},{6,7},{7,6},{8,9},{9,8},{10,11... | collective-permute-start | bytes 7962632 | tf_op jit(solution)/shard_map/ppermute | solution.py:41
  46.4 14.1 %collective-permute-start.11 = (bf16[80,3072]{1,0:T(8,128)(2,1)S(1)}, bf16[80,3072]{1,0:T(8,128)(2,1)S(1)}, u32[]{:S(2)}, u32[]{:S(2)}) collective-permute-start(bf16[80,3072]{1,0:T(8,128)(2,1)S(1)} %slice.12), channel_id=1, source_target_pairs={{0,2},{1,3},{2,4},{3,5},{4,6},{5,7},{6,0},{7,1},{8,10},{9,11},{10,... | collective-permute-start | bytes 1474568 | tf_op jit(solution)/shard_map/ppermute | solution.py:41
  47.6 14.0 %collective-permute-start.12 = (bf16[64,3072]{1,0:T(8,128)(2,1)S(1)}, bf16[64,3072]{1,0:T(8,128)(2,1)S(1)}, u32[]{:S(2)}, u32[]{:S(2)}) collective-permute-start(bf16[64,3072]{1,0:T(8,128)(2,1)S(1)} %slice.13), channel_id=1, source_target_pairs={{0,6},{1,7},{2,0},{3,1},{4,2},{5,3},{6,4},{7,5},{8,14},{9,15},{10,... | collective-permute-start | bytes 1179656 | tf_op jit(solution)/shard_map/ppermute | solution.py:41
  49.4 27.6 %collective-permute-start.10 = (bf16[144,3072]{1,0:T(8,128)(2,1)S(1)}, bf16[144,3072]{1,0:T(8,128)(2,1)S(1)}, u32[]{:S(2)}, u32[]{:S(2)}) collective-permute-start(bf16[144,3072]{1,0:T(8,128)(2,1)S(1)} %pad_maximum_fusion.3.refs_0_), channel_id=1, source_target_pairs={{0,6},{1,7},{2,0},{3,1},{4,2},{5,3},{6,4},{7,5},{8,14},{9,15},{10,... | collective-permute-start | bytes 2654216 | tf_op jit(solution)/shard_map/ppermute | solution.py:41
  50.8 28.6 %collective-permute-start.9 = (bf16[144,3072]{1,0:T(8,128)(2,1)S(1)}, bf16[144,3072]{1,0:T(8,128)(2,1)S(1)}, u32[]{:S(2)}, u32[]{:S(2)}) collective-permute-start(bf16[144,3072]{1,0:T(8,128)(2,1)S(1)} %pad_maximum_fusion.3.refs_0_), channel_id=1, source_target_pairs={{0,2},{1,3},{2,4},{3,5},{4,6},{5,7},{6,0},{7,1},{8,10},{9,11},{10,... | collective-permute-start | bytes 2654216 | tf_op jit(solution)/shard_map/ppermute | solution.py:41
  60.5 7.9 %collective-permute-start.13 = (bf16[80,3072]{1,0:T(8,128)(2,1)S(1)}, bf16[80,3072]{1,0:T(8,128)(2,1)S(1)}, u32[]{:S(2)}, u32[]{:S(2)}) collective-permute-start(bf16[80,3072]{1,0:T(8,128)(2,1)S(1)} %collective-permute-done.11.refs_0_), channel_id=1, source_target_pairs={{0,1},{1,0},{2,3},{3,2},{4,5},{5,4},{6,7},{7,6},{8,9},{9,8},{10,11... | collective-permute-start | bytes 1474568 | tf_op jit(solution)/shard_map/ppermute | solution.py:41
  61.7 6.7 %collective-permute-start.14 = (bf16[64,3072]{1,0:T(8,128)(2,1)S(1)}, bf16[64,3072]{1,0:T(8,128)(2,1)S(1)}, u32[]{:S(2)}, u32[]{:S(2)}) collective-permute-start(bf16[64,3072]{1,0:T(8,128)(2,1)S(1)} %collective-permute-done.12.refs_1_), channel_id=1, source_target_pairs={{0,1},{1,0},{2,3},{3,2},{4,5},{5,4},{6,7},{7,6},{8,9},{9,8},{10,11... | collective-permute-start | bytes 1179656 | tf_op jit(solution)/shard_map/ppermute | solution.py:41
  79.6 5.5 %collective-permute-start.18 = (bf16[432,3072]{1,0:T(8,128)(2,1)S(1)}, bf16[432,3072]{1,0:T(8,128)(2,1)S(1)}, u32[]{:S(2)}, u32[]{:S(2)}) collective-permute-start(bf16[432,3072]{1,0:T(8,128)(2,1)S(1)} %pad_maximum_fusion.1), channel_id=1, source_target_pairs={{0,1},{1,0},{2,3},{3,2},{4,5},{5,4},{6,7},{7,6},{8,9},{9,8},{10,11... | collective-permute-start | bytes 7962632 | tf_op jit(solution)/shard_map/ppermute | solution.py:41
  80.5 14.1 %collective-permute-start.16 = (bf16[80,3072]{1,0:T(8,128)(2,1)S(1)}, bf16[80,3072]{1,0:T(8,128)(2,1)S(1)}, u32[]{:S(2)}, u32[]{:S(2)}) collective-permute-start(bf16[80,3072]{1,0:T(8,128)(2,1)S(1)} %slice.14), channel_id=1, source_target_pairs={{0,2},{1,3},{2,4},{3,5},{4,6},{5,7},{6,0},{7,1},{8,10},{9,11},{10,... | collective-permute-start | bytes 1474568 | tf_op jit(solution)/shard_map/ppermute | solution.py:41
  80.7 11.2 %collective-permute-start.17 = (bf16[64,3072]{1,0:T(8,128)(2,1)S(1)}, bf16[64,3072]{1,0:T(8,128)(2,1)S(1)}, u32[]{:S(2)}, u32[]{:S(2)}) collective-permute-start(bf16[64,3072]{1,0:T(8,128)(2,1)S(1)} %slice.15), channel_id=1, source_target_pairs={{0,6},{1,7},{2,0},{3,1},{4,2},{5,3},{6,4},{7,5},{8,14},{9,15},{10,... | collective-permute-start | bytes 1179656 | tf_op jit(solution)/shard_map/ppermute | solution.py:41
  94.7 2.9 %collective-permute-start.19 = (bf16[80,3072]{1,0:T(8,128)(2,1)S(1)}, bf16[80,3072]{1,0:T(8,128)(2,1)S(1)}, u32[]{:S(2)}, u32[]{:S(2)}) collective-permute-start(bf16[80,3072]{1,0:T(8,128)(2,1)S(1)} %collective-permute-done.16.refs_0_), channel_id=1, source_target_pairs={{0,1},{1,0},{2,3},{3,2},{4,5},{5,4},{6,7},{7,6},{8,9},{9,8},{10,11... | collective-permute-start | bytes 1474568 | tf_op jit(solution)/shard_map/ppermute | solution.py:41
  95.5 2.1 %collective-permute-start.20 = (bf16[64,3072]{1,0:T(8,128)(2,1)S(1)}, bf16[64,3072]{1,0:T(8,128)(2,1)S(1)}, u32[]{:S(2)}, u32[]{:S(2)}) collective-permute-start(bf16[64,3072]{1,0:T(8,128)(2,1)S(1)} %collective-permute-done.17.refs_1_), channel_id=1, source_target_pairs={{0,1},{1,0},{2,3},{3,2},{4,5},{5,4},{6,7},{7,6},{8,9},{9,8},{10,11... | collective-permute-start | bytes 1179656 | tf_op jit(solution)/shard_map/ppermute | solution.py:41
  (6 other events, 92.8 us)
